TPU v7x, 512 devices: a whole 4x8x8 slice. The times are simulated.
512 devices in a mesh: dom: 64 (over y, z), gz: 8 (over x, core).
Axes of the slice: x: 4, y: 8, z: 8, core: 2. Of those that a mesh axis runs over, the one named last changes fastest.
Arguments:
- features: float32 [65536, 128], P(('dom', 'gz')), may hold values from -6 to 6
- positions: float32 [3, 65536], P(None, ('dom', 'gz')), may hold values from 0 to 1
- send_ids: int32 [512, 608], P(('dom', 'gz')), may hold values from 0 to 127
- ghost_prefix: int32 [512, 27], P(('dom', 'gz')), may hold values from 0 to 608, as said below
- edge_fill: int32 [512], P(('dom', 'gz')), may hold values from 128 to 512, as said below
- edge_src: int32 [512, 512], P(('dom', 'gz')), may hold values from 0 to 127
- edge_dst: int32 [512, 512], P(('dom', 'gz')), may hold values from 0 to 735, as said below
- weight_src: bfloat16 [128, 128], replicated, may hold values from -0.5 to 0.5
- weight_dst: bfloat16 [128, 128], replicated, may hold values from -0.5 to 0.5
- weight_radial: bfloat16 [8, 128], replicated, may hold values from -2 to 2
- weight_env: bfloat16 [128, 128], replicated, may hold values from -0.5 to 0.5
- weight_latent: bfloat16 [512, 128], replicated, may hold values from -0.25 to 0.25
- weight_hidden: bfloat16 [128, 128], replicated, may hold values from -0.5 to 0.5
- weight_readout: float32 [128], replicated, may hold values from -0.5 to 0.5
Outputs:
- forces: float32 [3, 65536], P(None, ('dom', 'gz'))
- feat_grad: float32 [65536, 128], P(('dom', 'gz'))
Inputs may be any that keep to these rules, and one draw needn't show every extreme that they name: `ghost_prefix`: each row starts at 0 and rises; the count of direction n lies between cap_n - cap_n // 2 and cap_n, and on one domain every count equals its capacity. `edge_fill`: A multiple of 128, at least 128 * max(512 // 512, 1); one domain uses all 512 slots. `edge_dst`: never equal to edge_src.
All inputs are finite; a program needn't handle non-finite values.
Results may differ from a plain program's by a relative error of at most 0.015.
Values sent between devices are 32-bit elements; how exact they have to be, the bound alone decides.
A program may use at most 64 MiB of HBM per device.

v0:
```python
import math

import jax
import jax.numpy as jnp
import numpy as np
from jax import lax
from jax.sharding import PartitionSpec as P

NEIGHBOURS = 4
CAP_FACE = 64
CAP_EDGE = 16
CAP_CORNER = 4


CUTOFF = 1.0
SHARPNESS = 8.0


def shifted(value, axis, steps):
    count = lax.axis_size(axis)
    pairs = [(source, (source + steps) % count) for source in range(count)]
    return lax.ppermute(value, axis, pairs)


def direction_table(face_cap, edge_cap, corner_cap):
    vectors = []
    capacity = []
    for first in (-1, 0, 1):
        for second in (-1, 0, 1):
            for third in (-1, 0, 1):
                nonzero = abs(first) + abs(second) + abs(third)
                if nonzero > 0:
                    vectors.append((first, second, third))
                    capacity.append((0, face_cap, edge_cap, corner_cap)[nonzero])
    offsets = np.concatenate([[0], np.cumsum(capacity)]).astype(np.int64)
    slot_dir = np.repeat(np.arange(26), capacity)
    slot_index = np.concatenate([np.arange(width) for width in capacity])
    return (np.array(vectors), capacity, offsets, slot_dir, slot_index)


def harmonics(scaled):
    x_part, y_part, z_part = (scaled[0], scaled[1], scaled[2])
    root_three = math.sqrt(3.0)
    root_fifteen = math.sqrt(15.0)
    root_five = math.sqrt(5.0)
    return jnp.stack(
        [
            jnp.ones_like(x_part),
            root_three * x_part,
            root_three * y_part,
            root_three * z_part,
            root_fifteen * x_part * y_part,
            root_fifteen * y_part * z_part,
            root_fifteen * z_part * x_part,
            0.5 * root_fifteen * (x_part * x_part - y_part * y_part),
            0.5 * root_five * (2.0 * z_part * z_part - x_part * x_part - y_part * y_part),
        ]
    )


def local_energy(
    node_pos,
    node_feat,
    node_live,
    edge_source,
    edge_target,
    fill,
    own_count,
    norm,
    weight_src,
    weight_dst,
    weight_radial,
    weight_env,
    weight_latent,
    weight_hidden,
    weight_readout,
):
    half_feat = node_feat.astype(jnp.bfloat16)
    proj_source = jnp.dot(half_feat[:own_count], weight_src, preferred_element_type=jnp.float32)
    proj_target = jnp.dot(half_feat, weight_dst, preferred_element_type=jnp.float32)
    relative = jnp.take(node_pos, edge_target, axis=1) - jnp.take(node_pos, edge_source, axis=1)
    scaled = relative / CUTOFF
    radius_sq = jnp.sum(scaled * scaled, axis=0)
    edge_total = edge_source.shape[0]
    in_use = (jnp.arange(edge_total) < fill).astype(jnp.float32) * node_live[edge_target]
    inside = radius_sq < 1.0
    envelope = jnp.where(inside, jnp.square(1.0 - jnp.minimum(radius_sq, 1.0)), 0.0) * in_use
    basis_count = weight_radial.shape[0]
    centers = jnp.arange(basis_count).astype(jnp.float32) / (basis_count - 1)
    radial_basis = jnp.exp(-SHARPNESS * jnp.square(radius_sq[None, :] - centers[:, None])).astype(
        jnp.bfloat16
    )
    radial = lax.dot_general(
        radial_basis, weight_radial, (((0,), (0,)), ((), ())), preferred_element_type=jnp.float32
    )
    pre_act = proj_source[edge_source] + proj_target[edge_target] + radial
    latent = (jax.nn.silu(pre_act) * envelope[:, None]).astype(jnp.bfloat16)
    env_weight = jnp.dot(latent, weight_env, preferred_element_type=jnp.float32)
    channels = env_weight.shape[1]
    harmonic = harmonics(scaled)
    harmonic_rows = jnp.transpose(harmonic)
    weighted = (harmonic_rows[:, :, None] * env_weight[:, None, :]).reshape(
        edge_total, 9 * channels
    )
    environment = jax.ops.segment_sum(weighted, edge_source, num_segments=own_count) / norm
    gathered = environment[edge_source].reshape(edge_total, 9, channels)
    scalar_parts = []
    for lower, upper in ((0, 1), (1, 4), (4, 9)):
        scalar_parts.append(
            jnp.sum(harmonic_rows[:, lower:upper, None] * gathered[:, lower:upper, :], axis=1)
        )
    scalars = jnp.concatenate(scalar_parts, axis=1).astype(jnp.bfloat16)
    joined = jnp.concatenate([latent, scalars], axis=1)
    update = jnp.dot(joined, weight_latent, preferred_element_type=jnp.float32)
    updated = (latent.astype(jnp.float32) + jax.nn.silu(update)).astype(jnp.bfloat16)
    hidden = jax.nn.silu(jnp.dot(updated, weight_hidden, preferred_element_type=jnp.float32))
    edge_energy = jnp.dot(hidden, weight_readout, precision=lax.Precision.HIGHEST) * envelope
    return jnp.sum(edge_energy)


def split_pieces(feat_rows, pos_rows, offsets):
    pieces = []
    for index in range(26):
        lower = int(offsets[index])
        upper = int(offsets[index + 1])
        pieces.append((feat_rows[lower:upper], pos_rows[:, lower:upper]))
    return pieces


def join_pieces(pieces):
    return (
        jnp.concatenate([piece[0] for piece in pieces], axis=0),
        jnp.concatenate([piece[1] for piece in pieces], axis=1),
    )


def plane_amounts(step_x, step_y, row_domains):
    base = step_x * row_domains
    if step_y == 0:
        return [base]
    return [base + step_y, base + step_y - step_y * row_domains]


def plane_pick(results, step_y, row_domains):
    if len(results) == 1:
        return results[0]
    place = lax.axis_index("dom") % row_domains
    at_edge = place == 0 if step_y > 0 else place == row_domains - 1
    inner = results[0]
    outer = results[1]
    return (jnp.where(at_edge, outer[0], inner[0]), jnp.where(at_edge, outer[1], inner[1]))


def ghosts_each(feat_rows, pos_rows, offsets, vectors, row_domains):
    pieces = split_pieces(feat_rows, pos_rows, offsets)
    moved = []
    for index in range(26):
        step_x = int(vectors[index][0])
        step_y = int(vectors[index][1])
        step_z = int(vectors[index][2])
        current = pieces[index]
        if step_z != 0:
            current = shifted((current[0], current[1]), "gz", step_z)
        if step_x != 0 or step_y != 0:
            results = []
            for amount in plane_amounts(step_x, step_y, row_domains):
                results.append(shifted((current[0], current[1]), "dom", amount))
            current = plane_pick(results, step_y, row_domains)
        moved.append(current)
    return join_pieces(moved)


def returns_each(feat_rows, pos_rows, offsets, vectors, row_domains):
    pieces = split_pieces(feat_rows, pos_rows, offsets)
    moved = []
    for index in range(26):
        step_x = -int(vectors[index][0])
        step_y = -int(vectors[index][1])
        step_z = -int(vectors[index][2])
        current = pieces[index]
        if step_x != 0 or step_y != 0:
            results = []
            for amount in plane_amounts(step_x, step_y, row_domains):
                results.append(shifted((current[0], current[1]), "dom", amount))
            current = plane_pick(results, step_y, row_domains)
        if step_z != 0:
            current = shifted((current[0], current[1]), "gz", step_z)
        moved.append(current)
    return join_pieces(moved)


def body(
    features,
    positions,
    send_ids,
    ghost_prefix,
    edge_fill,
    edge_src,
    edge_dst,
    weight_src,
    weight_dst,
    weight_radial,
    weight_env,
    weight_latent,
    weight_hidden,
    weight_readout,
):
    own_count = features.shape[0]
    vectors, capacity, offsets, slot_dir, slot_index = direction_table(
        CAP_FACE, CAP_EDGE, CAP_CORNER
    )
    row_domains = lax.axis_size("dom") // 8
    slot_dir_arr = jnp.array(slot_dir).astype(jnp.int32)
    slot_index_arr = jnp.array(slot_index).astype(jnp.int32)
    slot_vec = jnp.array(vectors[slot_dir].T).astype(jnp.float32)
    prefix = ghost_prefix[0]
    counts = prefix[1:] - prefix[:-1]
    live_slot = (slot_index_arr < counts[slot_dir_arr]).astype(jnp.float32)
    list_start = prefix[slot_dir_arr] + slot_index_arr
    owner_row = send_ids[0, list_start]
    send_feat = features[owner_row]
    send_pos = jnp.concatenate(
        [positions[:, owner_row] * live_slot[None, :], live_slot[None, :]], axis=0
    )
    arrived_feat, ghost_block = ghosts_each(send_feat, send_pos, offsets, vectors, row_domains)
    ghost_live = ghost_block[3]
    ghost_pos = ghost_block[:3] - slot_vec
    node_pos = jnp.concatenate([positions, ghost_pos], axis=1)
    node_live = jnp.concatenate([jnp.ones((own_count,), jnp.float32), ghost_live])
    norm = float(NEIGHBOURS)

    def energy_of(pos_in, own_in, arrived_in):
        feat_in = jnp.concatenate([own_in, arrived_in * ghost_live[:, None]], axis=0)
        return local_energy(
            pos_in,
            feat_in,
            node_live,
            edge_src[0],
            edge_dst[0],
            edge_fill[0],
            own_count,
            norm,
            weight_src,
            weight_dst,
            weight_radial,
            weight_env,
            weight_latent,
            weight_hidden,
            weight_readout,
        )

    energy, pullback = jax.vjp(energy_of, node_pos, features, arrived_feat)
    grad_pos, own_feat_grad, ghost_feat_grad = pullback(jnp.ones_like(energy))
    ghost_pos_grad = grad_pos[:, own_count:]
    back_feat, back_pos = returns_each(
        ghost_feat_grad, ghost_pos_grad, offsets, vectors, row_domains
    )
    returned_feat = jax.ops.segment_sum(
        back_feat * live_slot[:, None], owner_row, num_segments=own_count
    )
    returned_pos = jax.ops.segment_sum(
        back_pos.T * live_slot[:, None], owner_row, num_segments=own_count
    )
    forces = -(grad_pos[:, :own_count] + returned_pos.T)
    feat_grad = own_feat_grad + returned_feat
    return (forces, feat_grad)


def solution(mesh):
    return jax.shard_map(
        body,
        mesh=mesh,
        in_specs=(
            P(("dom", "gz"), None),
            P(None, ("dom", "gz")),
            P(("dom", "gz"), None),
            P(("dom", "gz"), None),
            P(("dom", "gz")),
            P(("dom", "gz"), None),
            P(("dom", "gz"), None),
            P(),
            P(),
            P(),
            P(),
            P(),
            P(),
            P(),
        ),
        out_specs=(P(None, ("dom", "gz")), P(("dom", "gz"), None)),
        check_vma=False,
    )
```

profile of v0, /device:TPU:1, one launch (start us, length us, event | category | flops | bytes accessed | tf_op | source)
XLA Modules:
  0.0 868.7 jit_solution(13675994340609509517)
XLA Ops:
  6.5 17.1 %fusion.70 = f32[608]{0:T(1024)S(1)} fusion(s32[608]{0:T(1024)} %constant.173.clone, pred[608]{0:T(1024)(128)(4,1)} %constant.285, pred[608]{0:T(1024)(128)(4,1)} %constant.286, pred[608]{0:T(1024)(128)(4,1)} %constant.287, pred[608]{0:T(1024)(128)(4,1)} %constant.288, pred[608]{0:T(1024)(128)(4,1)} %constant.289, pred[608]{0:T(1024)(128)(4,1)} %constant.290, ...), kind=kLoop, calls=%fused_computation.179 | loop fusion | flops 16416 | bytes 20168 | tf_op jit(solution)/shard_map/convert_element_type | solution.py:218
  23.7 17.0 %fusion.69 = s32[608]{0:T(1024)S(1)} fusion(s32[608]{0:T(1024)} %constant.173.clone, pred[608]{0:T(1024)(128)(4,1)} %constant.285, pred[608]{0:T(1024)(128)(4,1)} %constant.286, pred[608]{0:T(1024)(128)(4,1)} %constant.287, pred[608]{0:T(1024)(128)(4,1)} %constant.288, pred[608]{0:T(1024)(128)(4,1)} %constant.289, pred[608]{0:T(1024)(128)(4,1)} %constant.290, ...), kind=kLoop, calls=%fused_computation.170 | loop fusion | flops 18848 | bytes 20168 | tf_op jit(solution)/shard_map/concatenate | solution.py:220
  40.7 4.0 gather_fusion
  47.0 14.4 %collective-permute-start.25 = (f32[4,64]{1,0:T(4,128)S(1)}, f32[4,64]{1,0:T(4,128)S(1)}, u32[]{:S(2)}, u32[]{:S(2)}) collective-permute-start(f32[4,64]{1,0:T(4,128)S(1)} %get-tuple-element.135), channel_id=1, source_target_pairs={{0,504},{8,0},{16,8},{24,16},{32,24},{40,32},{48,40},{56,48},{64,5... | collective-permute-start | bytes 3080 | tf_op jit(solution)/shard_map/ppermute | solution.py:22
  94.4 4.3 collective-permute-start.45
  98.7 4.1 collective-permute-start.5
  108.0 4.1 collective-permute-start.13
  112.1 5.8 collective-permute-start.7
  132.4 4.7 collective-permute-start.20
  140.4 4.2 collective-permute-start.41
  146.9 5.5 collective-permute-start.42
  158.1 5.9 collective-permute-start.4
  172.2 6.0 collective-permute-start.26
  182.2 6.3 collective-permute-start.28
  207.6 5.7 collective-permute-start.23
  219.8 4.4 collective-permute-start.47
  232.7 4.6 collective-permute-start.9
  239.3 4.6 collective-permute-start.10
  284.3 5.1 collective-permute-start.105
  291.6 4.2 collective-permute-start.100
  297.7 4.6 collective-permute-start.80
  302.3 4.5 collective-permute-start.79
  308.8 7.4 collective-permute-start.74
  326.3 4.8 collective-permute-start.62
  331.2 4.6 collective-permute-start.61
  339.1 4.5 collective-permute-start.77
  346.0 4.9 collective-permute-start.64
  371.3 5.7 collective-permute-start.97
  379.1 4.5 collective-permute-start.92
  403.7 4.3 collective-permute-start.68
  415.7 4.6 collective-permute-start.72
  425.2 4.7 collective-permute-start.70
  440.0 6.6 scatter_custom_fusion
  457.2 6.4 scatter_custom_fusion.1
  486.3 5.0 collective-permute-start.173
  493.6 4.5 collective-permute-start.165
  502.9 5.1 collective-permute-start.159
  514.6 4.3 collective-permute-start.134
  522.0 4.0 collective-permute-start.126
  530.4 5.0 collective-permute-start.120
  535.4 4.1 collective-permute-start.176
  548.2 10.0 %collective-permute-start.179 = (f32[3,4]{0,1:T(4,128)S(1)}, f32[3,4]{0,1:T(4,128)S(1)}, u32[]{:S(2)}, u32[]{:S(2)}) collective-permute-start(f32[3,4]{0,1:T(4,128)S(1)} %broadcast_select_fusion.30), channel_id=1, source_target_pairs={{0,7},{1,0},{2,1},{3,2},{4,3},{5,4},{6,5},{7,6},{8,15},{9,8},{10,9... | collective-permute-start | bytes 152 | tf_op jit(solution)/shard_map/ppermute | solution.py:22
  576.8 4.9 collective-permute-start.157
  584.2 4.5 collective-permute-start.152
  592.7 5.5 collective-permute-start.146
  608.9 5.3 collective-permute-start.124
  616.1 6.7 collective-permute-start.155
  635.9 8.9 %collective-permute-start.171 = (f32[3,16]{0,1:T(8,128)S(1)}, f32[3,16]{0,1:T(8,128)S(1)}, u32[]{:S(2)}, u32[]{:S(2)}) collective-permute-start(f32[3,16]{0,1:T(8,128)S(1)} %collective-permute-done.170), channel_id=1, source_target_pairs={{0,7},{1,0},{2,1},{3,2},{4,3},{5,4},{6,5},{7,6},{8,15},{9,8},{10,9... | collective-permute-start | bytes 584 | tf_op jit(solution)/shard_map/ppermute | solution.py:22
  660.7 4.4 collective-permute-start.144
  665.2 5.6 collective-permute-start.238
  687.8 4.1 collective-permute-start.225
  692.3 6.0 scatter_custom_fusion.4
  699.1 5.5 collective-permute-start.224
  713.0 5.2 collective-permute-start.198
  723.4 4.3 collective-permute-start.186
  733.0 4.0 collective-permute-start.180
  737.1 5.7 collective-permute-start.236
  750.8 5.4 collective-permute-start.217
  766.4 4.5 collective-permute-start.206
  770.9 8.8 %collective-permute-start.239 = (f32[4,128]{1,0:T(4,128)S(1)}, f32[4,128]{1,0:T(4,128)S(1)}, u32[]{:S(2)}, u32[]{:S(2)}) collective-permute-start(f32[4,128]{1,0:T(4,128)S(1)} %broadcast_select_fusion.46), channel_id=1, source_target_pairs={{0,7},{1,0},{2,1},{3,2},{4,3},{5,4},{6,5},{7,6},{8,15},{9,8},{10,9... | collective-permute-start | bytes 6152 | tf_op jit(solution)/shard_map/ppermute | solution.py:22
  821.6 4.7 collective-permute-start.231
  826.3 6.0 collective-permute-start.215
  832.3 4.2 collective-permute-start.214
  861.0 6.7 scatter_custom_fusion.7
  (672 shorter events, 495.9 us)
Async XLA Ops:
  47.0 181.9 %collective-permute-start.25 = (f32[4,64]{1,0:T(4,128)S(1)}, f32[4,64]{1,0:T(4,128)S(1)}, u32[]{:S(2)}, u32[]{:S(2)}) collective-permute-start(f32[4,64]{1,0:T(4,128)S(1)} %get-tuple-element.135), channel_id=1, source_target_pairs={{0,504},{8,0},{16,8},{24,16},{32,24},{40,32},{48,40},{56,48},{64,5... | collective-permute-start | bytes 3080 | tf_op jit(solution)/shard_map/ppermute | solution.py:22
  61.4 167.5 %collective-permute-start.24 = (f32[4,64]{1,0:T(4,128)S(1)}, f32[4,64]{1,0:T(4,128)S(1)}, u32[]{:S(2)}, u32[]{:S(2)}) collective-permute-start(f32[4,64]{1,0:T(4,128)S(1)} %get-tuple-element.135), channel_id=1, source_target_pairs={{0,56},{8,64},{16,72},{24,80},{32,88},{40,96},{48,104},{56,112},{6... | collective-permute-start | bytes 3080 | tf_op jit(solution)/shard_map/ppermute | solution.py:22
  64.3 18.9 %collective-permute-start.44 = (f32[4,4]{1,0:T(4,128)S(1)}, f32[4,4]{1,0:T(4,128)S(1)}, u32[]{:S(2)}, u32[]{:S(2)}) collective-permute-start(f32[4,4]{1,0:T(4,128)S(1)} %get-tuple-element.126), channel_id=1, source_target_pairs={{0,1},{1,2},{2,3},{3,4},{4,5},{5,6},{6,7},{7,0},{8,9},{9,10},{10,1... | collective-permute-start | bytes 200 | tf_op jit(solution)/shard_map/ppermute | solution.py:22
  78.6 76.7 %collective-permute-start.43 = (f32[4,16]{1,0:T(4,128)S(1)}, f32[4,16]{1,0:T(4,128)S(1)}, u32[]{:S(2)}, u32[]{:S(2)}) collective-permute-start(f32[4,16]{1,0:T(4,128)S(1)} %get-tuple-element.131), channel_id=1, source_target_pairs={{0,56},{8,64},{16,72},{24,80},{32,88},{40,96},{48,104},{56,112},{6... | collective-permute-start | bytes 776 | tf_op jit(solution)/shard_map/ppermute | solution.py:22
  170.1 18.4 %collective-permute-start.16 = (f32[4,16]{1,0:T(4,128)S(1)}, f32[4,16]{1,0:T(4,128)S(1)}, u32[]{:S(2)}, u32[]{:S(2)}) collective-permute-start(f32[4,16]{1,0:T(4,128)S(1)} %get-tuple-element.123), channel_id=1, source_target_pairs={{0,392},{8,400},{16,408},{24,416},{32,424},{40,432},{48,440},{56,4... | collective-permute-start | bytes 776 | tf_op jit(solution)/shard_map/ppermute | solution.py:22
  204.7 40.8 %collective-permute-start.35 = (f32[4,64]{1,0:T(4,128)S(1)}, f32[4,64]{1,0:T(4,128)S(1)}, u32[]{:S(2)}, u32[]{:S(2)}) collective-permute-start(f32[4,64]{1,0:T(4,128)S(1)} %get-tuple-element.138), channel_id=1, source_target_pairs={{0,8},{8,16},{16,24},{24,32},{32,40},{40,48},{48,56},{56,64},{64,7... | collective-permute-start | bytes 3080 | tf_op jit(solution)/shard_map/ppermute | solution.py:22
  224.2 21.4 %collective-permute-start.34 = (f32[4,64]{1,0:T(4,128)S(1)}, f32[4,64]{1,0:T(4,128)S(1)}, u32[]{:S(2)}, u32[]{:S(2)}) collective-permute-start(f32[4,64]{1,0:T(4,128)S(1)} %get-tuple-element.138), channel_id=1, source_target_pairs={{0,456},{8,464},{16,472},{24,480},{32,488},{40,496},{48,504},{56,0... | collective-permute-start | bytes 3080 | tf_op jit(solution)/shard_map/ppermute | solution.py:22
  250.2 93.4 %collective-permute-start.116 = (f32[16,128]{1,0:T(8,128)S(1)}, f32[16,128]{1,0:T(8,128)S(1)}, u32[]{:S(2)}, u32[]{:S(2)}) collective-permute-start(f32[16,128]{1,0:T(8,128)S(1)} %get-tuple-element.87), channel_id=1, source_target_pairs={{0,72},{8,80},{16,88},{24,96},{32,104},{40,112},{48,120},{56,128},... | collective-permute-start | bytes 24584 | tf_op jit(solution)/shard_map/ppermute | solution.py:22
  252.2 93.9 %collective-permute-start.115 = (f32[16,128]{1,0:T(8,128)S(1)}, f32[16,128]{1,0:T(8,128)S(1)}, u32[]{:S(2)}, u32[]{:S(2)}) collective-permute-start(f32[16,128]{1,0:T(8,128)S(1)} %get-tuple-element.87), channel_id=1, source_target_pairs={{0,8},{8,16},{16,24},{24,32},{32,40},{40,48},{48,56},{56,64},{64,7... | collective-permute-start | bytes 24584 | tf_op jit(solution)/shard_map/ppermute | solution.py:22
  323.0 28.0 %collective-permute-start.103 = (f32[16,128]{1,0:T(8,128)S(1)}, f32[16,128]{1,0:T(8,128)S(1)}, u32[]{:S(2)}, u32[]{:S(2)}) collective-permute-start(f32[16,128]{1,0:T(8,128)S(1)} %get-tuple-element.90), channel_id=1, source_target_pairs={{0,56},{8,64},{16,72},{24,80},{32,88},{40,96},{48,104},{56,112},{6... | collective-permute-start | bytes 24584 | tf_op jit(solution)/shard_map/ppermute | solution.py:22
  335.7 17.8 %collective-permute-start.102 = (f32[16,128]{1,0:T(8,128)S(1)}, f32[16,128]{1,0:T(8,128)S(1)}, u32[]{:S(2)}, u32[]{:S(2)}) collective-permute-start(f32[16,128]{1,0:T(8,128)S(1)} %get-tuple-element.90), channel_id=1, source_target_pairs={{0,120},{8,128},{16,136},{24,144},{32,152},{40,160},{48,168},{56,1... | collective-permute-start | bytes 24584 | tf_op jit(solution)/shard_map/ppermute | solution.py:22
  339.1 17.2 %collective-permute-start.77 = (f32[16,128]{1,0:T(8,128)S(1)}, f32[16,128]{1,0:T(8,128)S(1)}, u32[]{:S(2)}, u32[]{:S(2)}) collective-permute-start(f32[16,128]{1,0:T(8,128)S(1)} %get-tuple-element.95), channel_id=1, source_target_pairs={{0,456},{8,464},{16,472},{24,480},{32,488},{40,496},{48,504},{56,0... | collective-permute-start | bytes 24584 | tf_op jit(solution)/shard_map/ppermute | solution.py:22
  346.0 23.4 %collective-permute-start.64 = (f32[16,128]{1,0:T(8,128)S(1)}, f32[16,128]{1,0:T(8,128)S(1)}, u32[]{:S(2)}, u32[]{:S(2)}) collective-permute-start(f32[16,128]{1,0:T(8,128)S(1)} %get-tuple-element.98), channel_id=1, source_target_pairs={{0,440},{8,448},{16,456},{24,464},{32,472},{40,480},{48,488},{56,4... | collective-permute-start | bytes 24584 | tf_op jit(solution)/shard_map/ppermute | solution.py:22
  351.0 20.3 %collective-permute-start.63 = (f32[16,128]{1,0:T(8,128)S(1)}, f32[16,128]{1,0:T(8,128)S(1)}, u32[]{:S(2)}, u32[]{:S(2)}) collective-permute-start(f32[16,128]{1,0:T(8,128)S(1)} %get-tuple-element.98), channel_id=1, source_target_pairs={{0,504},{8,0},{16,8},{24,16},{32,24},{40,32},{48,40},{56,48},{64,5... | collective-permute-start | bytes 24584 | tf_op jit(solution)/shard_map/ppermute | solution.py:22
  353.6 60.2 %collective-permute-start.95 = (f32[64,128]{1,0:T(8,128)S(1)}, f32[64,128]{1,0:T(8,128)S(1)}, u32[]{:S(2)}, u32[]{:S(2)}) collective-permute-start(f32[64,128]{1,0:T(8,128)S(1)} %get-tuple-element.100), channel_id=1, source_target_pairs={{0,8},{8,16},{16,24},{24,32},{32,40},{40,48},{48,56},{56,64},{64,7... | collective-permute-start | bytes 98312 | tf_op jit(solution)/shard_map/ppermute | solution.py:22
  356.3 59.4 %collective-permute-start.94 = (f32[64,128]{1,0:T(8,128)S(1)}, f32[64,128]{1,0:T(8,128)S(1)}, u32[]{:S(2)}, u32[]{:S(2)}) collective-permute-start(f32[64,128]{1,0:T(8,128)S(1)} %get-tuple-element.100), channel_id=1, source_target_pairs={{0,456},{8,464},{16,472},{24,480},{32,488},{40,496},{48,504},{56,0... | collective-permute-start | bytes 98312 | tf_op jit(solution)/shard_map/ppermute | solution.py:22
  408.0 17.3 %collective-permute-start.85 = (f32[64,128]{1,0:T(8,128)S(1)}, f32[64,128]{1,0:T(8,128)S(1)}, u32[]{:S(2)}, u32[]{:S(2)}) collective-permute-start(f32[64,128]{1,0:T(8,128)S(1)} %get-tuple-element.103), channel_id=1, source_target_pairs={{0,504},{8,0},{16,8},{24,16},{32,24},{40,32},{48,40},{56,48},{64,5... | collective-permute-start | bytes 98312 | tf_op jit(solution)/shard_map/ppermute | solution.py:22
  409.9 20.1 %collective-permute-start.84 = (f32[64,128]{1,0:T(8,128)S(1)}, f32[64,128]{1,0:T(8,128)S(1)}, u32[]{:S(2)}, u32[]{:S(2)}) collective-permute-start(f32[64,128]{1,0:T(8,128)S(1)} %get-tuple-element.103), channel_id=1, source_target_pairs={{0,56},{8,64},{16,72},{24,80},{32,88},{40,96},{48,104},{56,112},{6... | collective-permute-start | bytes 98312 | tf_op jit(solution)/shard_map/ppermute | solution.py:22
  480.7 17.3 %collective-permute-start.178 = (f32[3,4]{0,1:T(4,128)S(1)}, f32[3,4]{0,1:T(4,128)S(1)}, u32[]{:S(2)}, u32[]{:S(2)}) collective-permute-start(f32[3,4]{0,1:T(4,128)S(1)} %get-tuple-element.27), channel_id=1, source_target_pairs={{0,440},{8,448},{16,456},{24,464},{32,472},{40,480},{48,488},{56,4... | collective-permute-start | bytes 152 | tf_op jit(solution)/shard_map/ppermute | solution.py:22
  482.9 18.1 %collective-permute-start.177 = (f32[3,4]{0,1:T(4,128)S(1)}, f32[3,4]{0,1:T(4,128)S(1)}, u32[]{:S(2)}, u32[]{:S(2)}) collective-permute-start(f32[3,4]{0,1:T(4,128)S(1)} %get-tuple-element.27), channel_id=1, source_target_pairs={{0,504},{8,0},{16,8},{24,16},{32,24},{40,32},{48,40},{56,48},{64,5... | collective-permute-start | bytes 152 | tf_op jit(solution)/shard_map/ppermute | solution.py:22
  493.6 17.2 %collective-permute-start.165 = (f32[3,4]{0,1:T(4,128)S(1)}, f32[3,4]{0,1:T(4,128)S(1)}, u32[]{:S(2)}, u32[]{:S(2)}) collective-permute-start(f32[3,4]{0,1:T(4,128)S(1)} %get-tuple-element.29), channel_id=1, source_target_pairs={{0,456},{8,464},{16,472},{24,480},{32,488},{40,496},{48,504},{56,0... | collective-permute-start | bytes 152 | tf_op jit(solution)/shard_map/ppermute | solution.py:22
  501.0 18.0 %collective-permute-start.160 = (f32[3,4]{0,1:T(4,128)S(1)}, f32[3,4]{0,1:T(4,128)S(1)}, u32[]{:S(2)}, u32[]{:S(2)}) collective-permute-start(f32[3,4]{0,1:T(4,128)S(1)} %get-tuple-element.30), channel_id=1, source_target_pairs={{0,456},{8,464},{16,472},{24,480},{32,488},{40,496},{48,504},{56,0... | collective-permute-start | bytes 152 | tf_op jit(solution)/shard_map/ppermute | solution.py:22
  502.9 19.1 %collective-permute-start.159 = (f32[3,4]{0,1:T(4,128)S(1)}, f32[3,4]{0,1:T(4,128)S(1)}, u32[]{:S(2)}, u32[]{:S(2)}) collective-permute-start(f32[3,4]{0,1:T(4,128)S(1)} %get-tuple-element.30), channel_id=1, source_target_pairs={{0,392},{8,400},{16,408},{24,416},{32,424},{40,432},{48,440},{56,4... | collective-permute-start | bytes 152 | tf_op jit(solution)/shard_map/ppermute | solution.py:22
  508.1 18.0 %collective-permute-start.139 = (f32[3,4]{0,1:T(4,128)S(1)}, f32[3,4]{0,1:T(4,128)S(1)}, u32[]{:S(2)}, u32[]{:S(2)}) collective-permute-start(f32[3,4]{0,1:T(4,128)S(1)} %get-tuple-element.31), channel_id=1, source_target_pairs={{0,56},{8,64},{16,72},{24,80},{32,88},{40,96},{48,104},{56,112},{6... | collective-permute-start | bytes 152 | tf_op jit(solution)/shard_map/ppermute | solution.py:22
  510.8 17.3 %collective-permute-start.138 = (f32[3,4]{0,1:T(4,128)S(1)}, f32[3,4]{0,1:T(4,128)S(1)}, u32[]{:S(2)}, u32[]{:S(2)}) collective-permute-start(f32[3,4]{0,1:T(4,128)S(1)} %get-tuple-element.31), channel_id=1, source_target_pairs={{0,120},{8,128},{16,136},{24,144},{32,152},{40,160},{48,168},{56,1... | collective-permute-start | bytes 152 | tf_op jit(solution)/shard_map/ppermute | solution.py:22
  522.0 17.5 %collective-permute-start.126 = (f32[3,4]{0,1:T(4,128)S(1)}, f32[3,4]{0,1:T(4,128)S(1)}, u32[]{:S(2)}, u32[]{:S(2)}) collective-permute-start(f32[3,4]{0,1:T(4,128)S(1)} %get-tuple-element.33), channel_id=1, source_target_pairs={{0,72},{8,80},{16,88},{24,96},{32,104},{40,112},{48,120},{56,128},... | collective-permute-start | bytes 152 | tf_op jit(solution)/shard_map/ppermute | solution.py:22
  526.1 16.8 %collective-permute-start.125 = (f32[3,4]{0,1:T(4,128)S(1)}, f32[3,4]{0,1:T(4,128)S(1)}, u32[]{:S(2)}, u32[]{:S(2)}) collective-permute-start(f32[3,4]{0,1:T(4,128)S(1)} %get-tuple-element.33), channel_id=1, source_target_pairs={{0,8},{8,16},{16,24},{24,32},{32,40},{40,48},{48,56},{56,64},{64,7... | collective-permute-start | bytes 152 | tf_op jit(solution)/shard_map/ppermute | solution.py:22
  528.0 17.1 %collective-permute-start.121 = (f32[3,4]{0,1:T(4,128)S(1)}, f32[3,4]{0,1:T(4,128)S(1)}, u32[]{:S(2)}, u32[]{:S(2)}) collective-permute-start(f32[3,4]{0,1:T(4,128)S(1)} %get-tuple-element.34), channel_id=1, source_target_pairs={{0,72},{8,80},{16,88},{24,96},{32,104},{40,112},{48,120},{56,128},... | collective-permute-start | bytes 152 | tf_op jit(solution)/shard_map/ppermute | solution.py:22
  530.4 17.8 %collective-permute-start.120 = (f32[3,4]{0,1:T(4,128)S(1)}, f32[3,4]{0,1:T(4,128)S(1)}, u32[]{:S(2)}, u32[]{:S(2)}) collective-permute-start(f32[3,4]{0,1:T(4,128)S(1)} %get-tuple-element.34), channel_id=1, source_target_pairs={{0,8},{8,16},{16,24},{24,32},{32,40},{40,48},{48,56},{56,64},{64,7... | collective-permute-start | bytes 152 | tf_op jit(solution)/shard_map/ppermute | solution.py:22
  535.4 46.3 %collective-permute-start.176 = (f32[3,16]{0,1:T(8,128)S(1)}, f32[3,16]{0,1:T(8,128)S(1)}, u32[]{:S(2)}, u32[]{:S(2)}) collective-permute-start(f32[3,16]{0,1:T(8,128)S(1)} %get-tuple-element.35), channel_id=1, source_target_pairs={{0,440},{8,448},{16,456},{24,464},{32,472},{40,480},{48,488},{56,4... | collective-permute-start | bytes 584 | tf_op jit(solution)/shard_map/ppermute | solution.py:22
  539.5 44.7 %collective-permute-start.175 = (f32[3,16]{0,1:T(8,128)S(1)}, f32[3,16]{0,1:T(8,128)S(1)}, u32[]{:S(2)}, u32[]{:S(2)}) collective-permute-start(f32[3,16]{0,1:T(8,128)S(1)} %get-tuple-element.35), channel_id=1, source_target_pairs={{0,504},{8,0},{16,8},{24,16},{32,24},{40,32},{48,40},{56,48},{64,5... | collective-permute-start | bytes 584 | tf_op jit(solution)/shard_map/ppermute | solution.py:22
  542.9 45.9 %collective-permute-start.163 = (f32[3,16]{0,1:T(8,128)S(1)}, f32[3,16]{0,1:T(8,128)S(1)}, u32[]{:S(2)}, u32[]{:S(2)}) collective-permute-start(f32[3,16]{0,1:T(8,128)S(1)} %get-tuple-element.38), channel_id=1, source_target_pairs={{0,456},{8,464},{16,472},{24,480},{32,488},{40,496},{48,504},{56,0... | collective-permute-start | bytes 584 | tf_op jit(solution)/shard_map/ppermute | solution.py:22
  545.1 45.6 %collective-permute-start.162 = (f32[3,16]{0,1:T(8,128)S(1)}, f32[3,16]{0,1:T(8,128)S(1)}, u32[]{:S(2)}, u32[]{:S(2)}) collective-permute-start(f32[3,16]{0,1:T(8,128)S(1)} %get-tuple-element.38), channel_id=1, source_target_pairs={{0,392},{8,400},{16,408},{24,416},{32,424},{40,432},{48,440},{56,4... | collective-permute-start | bytes 584 | tf_op jit(solution)/shard_map/ppermute | solution.py:22
  598.2 35.6 %collective-permute-start.142 = (f32[3,16]{0,1:T(8,128)S(1)}, f32[3,16]{0,1:T(8,128)S(1)}, u32[]{:S(2)}, u32[]{:S(2)}) collective-permute-start(f32[3,16]{0,1:T(8,128)S(1)} %get-tuple-element.42), channel_id=1, source_target_pairs={{0,8},{8,16},{16,24},{24,32},{32,40},{40,48},{48,56},{56,64},{64,7... | collective-permute-start | bytes 584 | tf_op jit(solution)/shard_map/ppermute | solution.py:22
  600.1 35.8 %collective-permute-start.141 = (f32[3,16]{0,1:T(8,128)S(1)}, f32[3,16]{0,1:T(8,128)S(1)}, u32[]{:S(2)}, u32[]{:S(2)}) collective-permute-start(f32[3,16]{0,1:T(8,128)S(1)} %get-tuple-element.42), channel_id=1, source_target_pairs={{0,456},{8,464},{16,472},{24,480},{32,488},{40,496},{48,504},{56,0... | collective-permute-start | bytes 584 | tf_op jit(solution)/shard_map/ppermute | solution.py:22
  616.1 54.8 %collective-permute-start.155 = (f32[3,64]{0,1:T(8,128)S(1)}, f32[3,64]{0,1:T(8,128)S(1)}, u32[]{:S(2)}, u32[]{:S(2)}) collective-permute-start(f32[3,64]{0,1:T(8,128)S(1)} %get-tuple-element.48), channel_id=1, source_target_pairs={{0,504},{8,0},{16,8},{24,16},{32,24},{40,32},{48,40},{56,48},{64,5... | collective-permute-start | bytes 2312 | tf_op jit(solution)/shard_map/ppermute | solution.py:22
  622.9 50.0 %collective-permute-start.154 = (f32[3,64]{0,1:T(8,128)S(1)}, f32[3,64]{0,1:T(8,128)S(1)}, u32[]{:S(2)}, u32[]{:S(2)}) collective-permute-start(f32[3,64]{0,1:T(8,128)S(1)} %get-tuple-element.48), channel_id=1, source_target_pairs={{0,56},{8,64},{16,72},{24,80},{32,88},{40,96},{48,104},{56,112},{6... | collective-permute-start | bytes 2312 | tf_op jit(solution)/shard_map/ppermute | solution.py:22
  647.1 29.7 %collective-permute-start.145 = (f32[3,64]{0,1:T(8,128)S(1)}, f32[3,64]{0,1:T(8,128)S(1)}, u32[]{:S(2)}, u32[]{:S(2)}) collective-permute-start(f32[3,64]{0,1:T(8,128)S(1)} %get-tuple-element.51), channel_id=1, source_target_pairs={{0,8},{8,16},{16,24},{24,32},{32,40},{40,48},{48,56},{56,64},{64,7... | collective-permute-start | bytes 2312 | tf_op jit(solution)/shard_map/ppermute | solution.py:22
  665.2 33.9 %collective-permute-start.238 = (f32[4,128]{1,0:T(4,128)S(1)}, f32[4,128]{1,0:T(4,128)S(1)}, u32[]{:S(2)}, u32[]{:S(2)}) collective-permute-start(f32[4,128]{1,0:T(4,128)S(1)} %get-tuple-element.53), channel_id=1, source_target_pairs={{0,440},{8,448},{16,456},{24,464},{32,472},{40,480},{48,488},{56,4... | collective-permute-start | bytes 6152 | tf_op jit(solution)/shard_map/ppermute | solution.py:22
  680.6 23.9 %collective-permute-start.237 = (f32[4,128]{1,0:T(4,128)S(1)}, f32[4,128]{1,0:T(4,128)S(1)}, u32[]{:S(2)}, u32[]{:S(2)}) collective-permute-start(f32[4,128]{1,0:T(4,128)S(1)} %get-tuple-element.53), channel_id=1, source_target_pairs={{0,504},{8,0},{16,8},{24,16},{32,24},{40,32},{48,40},{56,48},{64,5... | collective-permute-start | bytes 6152 | tf_op jit(solution)/shard_map/ppermute | solution.py:22
  683.8 23.6 %collective-permute-start.233 = (f32[4,128]{1,0:T(4,128)S(1)}, f32[4,128]{1,0:T(4,128)S(1)}, u32[]{:S(2)}, u32[]{:S(2)}) collective-permute-start(f32[4,128]{1,0:T(4,128)S(1)} %get-tuple-element.54), channel_id=1, source_target_pairs={{0,440},{8,448},{16,456},{24,464},{32,472},{40,480},{48,488},{56,4... | collective-permute-start | bytes 6152 | tf_op jit(solution)/shard_map/ppermute | solution.py:22
  685.8 23.9 %collective-permute-start.232 = (f32[4,128]{1,0:T(4,128)S(1)}, f32[4,128]{1,0:T(4,128)S(1)}, u32[]{:S(2)}, u32[]{:S(2)}) collective-permute-start(f32[4,128]{1,0:T(4,128)S(1)} %get-tuple-element.54), channel_id=1, source_target_pairs={{0,504},{8,0},{16,8},{24,16},{32,24},{40,32},{48,40},{56,48},{64,5... | collective-permute-start | bytes 6152 | tf_op jit(solution)/shard_map/ppermute | solution.py:22
  687.8 25.2 %collective-permute-start.225 = (f32[4,128]{1,0:T(4,128)S(1)}, f32[4,128]{1,0:T(4,128)S(1)}, u32[]{:S(2)}, u32[]{:S(2)}) collective-permute-start(f32[4,128]{1,0:T(4,128)S(1)} %get-tuple-element.55), channel_id=1, source_target_pairs={{0,456},{8,464},{16,472},{24,480},{32,488},{40,496},{48,504},{56,0... | collective-permute-start | bytes 6152 | tf_op jit(solution)/shard_map/ppermute | solution.py:22
  699.1 19.1 %collective-permute-start.224 = (f32[4,128]{1,0:T(4,128)S(1)}, f32[4,128]{1,0:T(4,128)S(1)}, u32[]{:S(2)}, u32[]{:S(2)}) collective-permute-start(f32[4,128]{1,0:T(4,128)S(1)} %get-tuple-element.55), channel_id=1, source_target_pairs={{0,392},{8,400},{16,408},{24,416},{32,424},{40,432},{48,440},{56,4... | collective-permute-start | bytes 6152 | tf_op jit(solution)/shard_map/ppermute | solution.py:22
  709.7 18.0 %collective-permute-start.199 = (f32[4,128]{1,0:T(4,128)S(1)}, f32[4,128]{1,0:T(4,128)S(1)}, u32[]{:S(2)}, u32[]{:S(2)}) collective-permute-start(f32[4,128]{1,0:T(4,128)S(1)} %get-tuple-element.57), channel_id=1, source_target_pairs={{0,56},{8,64},{16,72},{24,80},{32,88},{40,96},{48,104},{56,112},{6... | collective-permute-start | bytes 6152 | tf_op jit(solution)/shard_map/ppermute | solution.py:22
  713.0 18.0 %collective-permute-start.198 = (f32[4,128]{1,0:T(4,128)S(1)}, f32[4,128]{1,0:T(4,128)S(1)}, u32[]{:S(2)}, u32[]{:S(2)}) collective-permute-start(f32[4,128]{1,0:T(4,128)S(1)} %get-tuple-element.57), channel_id=1, source_target_pairs={{0,120},{8,128},{16,136},{24,144},{32,152},{40,160},{48,168},{56,1... | collective-permute-start | bytes 6152 | tf_op jit(solution)/shard_map/ppermute | solution.py:22
  720.2 16.9 %collective-permute-start.193 = (f32[4,128]{1,0:T(4,128)S(1)}, f32[4,128]{1,0:T(4,128)S(1)}, u32[]{:S(2)}, u32[]{:S(2)}) collective-permute-start(f32[4,128]{1,0:T(4,128)S(1)} %get-tuple-element.58), channel_id=1, source_target_pairs={{0,120},{8,128},{16,136},{24,144},{32,152},{40,160},{48,168},{56,1... | collective-permute-start | bytes 6152 | tf_op jit(solution)/shard_map/ppermute | solution.py:22
  723.4 19.4 %collective-permute-start.186 = (f32[4,128]{1,0:T(4,128)S(1)}, f32[4,128]{1,0:T(4,128)S(1)}, u32[]{:S(2)}, u32[]{:S(2)}) collective-permute-start(f32[4,128]{1,0:T(4,128)S(1)} %get-tuple-element.59), channel_id=1, source_target_pairs={{0,72},{8,80},{16,88},{24,96},{32,104},{40,112},{48,120},{56,128},... | collective-permute-start | bytes 6152 | tf_op jit(solution)/shard_map/ppermute | solution.py:22
  727.7 18.3 %collective-permute-start.185 = (f32[4,128]{1,0:T(4,128)S(1)}, f32[4,128]{1,0:T(4,128)S(1)}, u32[]{:S(2)}, u32[]{:S(2)}) collective-permute-start(f32[4,128]{1,0:T(4,128)S(1)} %get-tuple-element.59), channel_id=1, source_target_pairs={{0,8},{8,16},{16,24},{24,32},{32,40},{40,48},{48,56},{56,64},{64,7... | collective-permute-start | bytes 6152 | tf_op jit(solution)/shard_map/ppermute | solution.py:22
  731.1 17.8 %collective-permute-start.181 = (f32[4,128]{1,0:T(4,128)S(1)}, f32[4,128]{1,0:T(4,128)S(1)}, u32[]{:S(2)}, u32[]{:S(2)}) collective-permute-start(f32[4,128]{1,0:T(4,128)S(1)} %get-tuple-element.60), channel_id=1, source_target_pairs={{0,72},{8,80},{16,88},{24,96},{32,104},{40,112},{48,120},{56,128},... | collective-permute-start | bytes 6152 | tf_op jit(solution)/shard_map/ppermute | solution.py:22
  733.0 17.7 %collective-permute-start.180 = (f32[4,128]{1,0:T(4,128)S(1)}, f32[4,128]{1,0:T(4,128)S(1)}, u32[]{:S(2)}, u32[]{:S(2)}) collective-permute-start(f32[4,128]{1,0:T(4,128)S(1)} %get-tuple-element.60), channel_id=1, source_target_pairs={{0,8},{8,16},{16,24},{24,32},{32,40},{40,48},{48,56},{56,64},{64,7... | collective-permute-start | bytes 6152 | tf_op jit(solution)/shard_map/ppermute | solution.py:22
  737.1 19.1 %collective-permute-start.236 = (f32[16,128]{1,0:T(8,128)S(1)}, f32[16,128]{1,0:T(8,128)S(1)}, u32[]{:S(2)}, u32[]{:S(2)}) collective-permute-start(f32[16,128]{1,0:T(8,128)S(1)} %get-tuple-element.61), channel_id=1, source_target_pairs={{0,440},{8,448},{16,456},{24,464},{32,472},{40,480},{48,488},{56,4... | collective-permute-start | bytes 24584 | tf_op jit(solution)/shard_map/ppermute | solution.py:22
  758.1 22.4 %collective-permute-start.212 = (f32[16,128]{1,0:T(8,128)S(1)}, f32[16,128]{1,0:T(8,128)S(1)}, u32[]{:S(2)}, u32[]{:S(2)}) collective-permute-start(f32[16,128]{1,0:T(8,128)S(1)} %get-tuple-element.66), channel_id=1, source_target_pairs={{0,504},{8,0},{16,8},{24,16},{32,24},{40,32},{48,40},{56,48},{64,5... | collective-permute-start | bytes 24584 | tf_op jit(solution)/shard_map/ppermute | solution.py:22
  761.5 19.6 %collective-permute-start.211 = (f32[16,128]{1,0:T(8,128)S(1)}, f32[16,128]{1,0:T(8,128)S(1)}, u32[]{:S(2)}, u32[]{:S(2)}) collective-permute-start(f32[16,128]{1,0:T(8,128)S(1)} %get-tuple-element.66), channel_id=1, source_target_pairs={{0,56},{8,64},{16,72},{24,80},{32,88},{40,96},{48,104},{56,112},{6... | collective-permute-start | bytes 24584 | tf_op jit(solution)/shard_map/ppermute | solution.py:22
  763.4 28.7 %collective-permute-start.207 = (f32[16,128]{1,0:T(8,128)S(1)}, f32[16,128]{1,0:T(8,128)S(1)}, u32[]{:S(2)}, u32[]{:S(2)}) collective-permute-start(f32[16,128]{1,0:T(8,128)S(1)} %get-tuple-element.67), channel_id=1, source_target_pairs={{0,8},{8,16},{16,24},{24,32},{32,40},{40,48},{48,56},{56,64},{64,7... | collective-permute-start | bytes 24584 | tf_op jit(solution)/shard_map/ppermute | solution.py:22
  766.4 25.7 %collective-permute-start.206 = (f32[16,128]{1,0:T(8,128)S(1)}, f32[16,128]{1,0:T(8,128)S(1)}, u32[]{:S(2)}, u32[]{:S(2)}) collective-permute-start(f32[16,128]{1,0:T(8,128)S(1)} %get-tuple-element.67), channel_id=1, source_target_pairs={{0,456},{8,464},{16,472},{24,480},{32,488},{40,496},{48,504},{56,0... | collective-permute-start | bytes 24584 | tf_op jit(solution)/shard_map/ppermute | solution.py:22
  782.3 22.1 %collective-permute-start.202 = (f32[16,128]{1,0:T(8,128)S(1)}, f32[16,128]{1,0:T(8,128)S(1)}, u32[]{:S(2)}, u32[]{:S(2)}) collective-permute-start(f32[16,128]{1,0:T(8,128)S(1)} %get-tuple-element.68), channel_id=1, source_target_pairs={{0,8},{8,16},{16,24},{24,32},{32,40},{40,48},{48,56},{56,64},{64,7... | collective-permute-start | bytes 24584 | tf_op jit(solution)/shard_map/ppermute | solution.py:22
  785.4 23.0 %collective-permute-start.201 = (f32[16,128]{1,0:T(8,128)S(1)}, f32[16,128]{1,0:T(8,128)S(1)}, u32[]{:S(2)}, u32[]{:S(2)}) collective-permute-start(f32[16,128]{1,0:T(8,128)S(1)} %get-tuple-element.68), channel_id=1, source_target_pairs={{0,456},{8,464},{16,472},{24,480},{32,488},{40,496},{48,504},{56,0... | collective-permute-start | bytes 24584 | tf_op jit(solution)/shard_map/ppermute | solution.py:22
  793.5 25.6 %collective-permute-start.197 = (f32[16,128]{1,0:T(8,128)S(1)}, f32[16,128]{1,0:T(8,128)S(1)}, u32[]{:S(2)}, u32[]{:S(2)}) collective-permute-start(f32[16,128]{1,0:T(8,128)S(1)} %get-tuple-element.69), channel_id=1, source_target_pairs={{0,56},{8,64},{16,72},{24,80},{32,88},{40,96},{48,104},{56,112},{6... | collective-permute-start | bytes 24584 | tf_op jit(solution)/shard_map/ppermute | solution.py:22
  796.6 25.0 %collective-permute-start.196 = (f32[16,128]{1,0:T(8,128)S(1)}, f32[16,128]{1,0:T(8,128)S(1)}, u32[]{:S(2)}, u32[]{:S(2)}) collective-permute-start(f32[16,128]{1,0:T(8,128)S(1)} %get-tuple-element.69), channel_id=1, source_target_pairs={{0,120},{8,128},{16,136},{24,144},{32,152},{40,160},{48,168},{56,1... | collective-permute-start | bytes 24584 | tf_op jit(solution)/shard_map/ppermute | solution.py:22
  813.1 23.4 %collective-permute-start.184 = (f32[16,128]{1,0:T(8,128)S(1)}, f32[16,128]{1,0:T(8,128)S(1)}, u32[]{:S(2)}, u32[]{:S(2)}) collective-permute-start(f32[16,128]{1,0:T(8,128)S(1)} %get-tuple-element.72), channel_id=1, source_target_pairs={{0,72},{8,80},{16,88},{24,96},{32,104},{40,112},{48,120},{56,128},... | collective-permute-start | bytes 24584 | tf_op jit(solution)/shard_map/ppermute | solution.py:22
  815.0 21.6 %collective-permute-start.183 = (f32[16,128]{1,0:T(8,128)S(1)}, f32[16,128]{1,0:T(8,128)S(1)}, u32[]{:S(2)}, u32[]{:S(2)}) collective-permute-start(f32[16,128]{1,0:T(8,128)S(1)} %get-tuple-element.72), channel_id=1, source_target_pairs={{0,8},{8,16},{16,24},{24,32},{32,40},{40,48},{48,56},{56,64},{64,7... | collective-permute-start | bytes 24584 | tf_op jit(solution)/shard_map/ppermute | solution.py:22
  826.3 21.4 %collective-permute-start.215 = (f32[64,128]{1,0:T(8,128)S(1)}, f32[64,128]{1,0:T(8,128)S(1)}, u32[]{:S(2)}, u32[]{:S(2)}) collective-permute-start(f32[64,128]{1,0:T(8,128)S(1)} %get-tuple-element.74), channel_id=1, source_target_pairs={{0,504},{8,0},{16,8},{24,16},{32,24},{40,32},{48,40},{56,48},{64,5... | collective-permute-start | bytes 98312 | tf_op jit(solution)/shard_map/ppermute | solution.py:22
  840.9 16.9 %collective-permute-start.204 = (f32[64,128]{1,0:T(8,128)S(1)}, f32[64,128]{1,0:T(8,128)S(1)}, u32[]{:S(2)}, u32[]{:S(2)}) collective-permute-start(f32[64,128]{1,0:T(8,128)S(1)} %get-tuple-element.77), channel_id=1, source_target_pairs={{0,456},{8,464},{16,472},{24,480},{32,488},{40,496},{48,504},{56,0... | collective-permute-start | bytes 98312 | tf_op jit(solution)/shard_map/ppermute | solution.py:22
  (193 other events, 2615.9 us)
where the time goes:
time: 882 us; the launch traced here: 869 us
  starting transfers between devices  699 us (79%)
  other arithmetic  73.6 us (8%)
  waiting for transfers between devices  46.3 us (5%)
  local copies, waits for them, and re-layouts  40.5 us (5%)
    ppermute x240, starting transfers between devices, shifted(): return lax.ppermute(value, axis, pairs)  699 us
    ppermute x240, waiting for transfers between devices, shifted(): return lax.ppermute(value, axis, pairs)  46.3 us
  transfers between devices with their start and end apart: 240, of which 33 were waited for; matrix products, arithmetic and copies ran while one was open for 2% of the time, Pallas kernels for 0%

commit v1 on v0

v1 whole, which is shorter than its diff:
```python
import math

import jax
import jax.numpy as jnp
import numpy as np
from jax import lax
from jax.experimental import pallas as pl
from jax.experimental.pallas import tpu as pltpu
from jax.sharding import PartitionSpec as P

NEIGHBOURS = 4
CAPS = (0, 64, 16, 4)
ROW_Y = 8

ATOMS = 128
EDGES = 512
CH = 128
SLOTS = 640
SHARPNESS = 8.0
VMEM = 56 * 1024 * 1024

BF16 = jnp.bfloat16
F32 = jnp.float32
MESH = pl.DeviceIdType.MESH


def directions():
    table = []
    offset = 0
    number = 0
    for a in (-1, 0, 1):
        for b in (-1, 0, 1):
            for c in (-1, 0, 1):
                kind = abs(a) + abs(b) + abs(c)
                if kind == 0:
                    continue
                cap = CAPS[kind]
                table.append(dict(vec=(a, b, c), kind=kind, cap=cap, number=number, offset=offset))
                offset += cap
                number += 1
    table.sort(key=lambda d: (d["kind"], d["number"]))
    row = 0
    slot = 0
    for d in table:
        d["rows"] = {1: 64, 2: 16, 3: 8}[d["kind"]]
        d["slot"] = slot
        d["at"] = row
        d["size"] = {1: 72, 2: 24, 3: 8}[d["kind"]]
        d["tile"] = row + {1: 64, 2: 16, 3: 0}[d["kind"]]
        slot += d["rows"]
        row += d["size"]
    assert slot == SLOTS
    return table, row


TABLE, PACK = directions()


def mm(a, b):
    return lax.dot_general(a, b, (((1,), (0,)), ((), ())), preferred_element_type=F32)


def nt(a, b):
    return lax.dot_general(a, b, (((1,), (1,)), ((), ())), preferred_element_type=F32)


def tn(a, b):
    return lax.dot_general(a, b, (((0,), (0,)), ((), ())), preferred_element_type=F32)


def iota(shape, dim):
    return lax.broadcasted_iota(jnp.int32, shape, dim)


def onehot(cond):
    return jnp.where(cond, 1.0, 0.0).astype(BF16)


def split(x, pieces):
    out = []
    for step in range(pieces):
        part = x.astype(BF16)
        out.append(part)
        if step + 1 < pieces:
            x = x - part.astype(F32)
    return out


def split_rows(x, pieces):
    parts = []
    for step in range(pieces):
        part = x.astype(BF16).astype(F32)
        parts.append(part)
        x = x - part
    if pieces % 2:
        parts.append(jnp.zeros_like(x))
    return jnp.concatenate(parts, axis=0).astype(BF16)


def sum_pieces(x, pieces):
    total = x[0:8]
    for step in range(1, pieces):
        total = total + x[8 * step : 8 * step + 8]
    return total


def sigmoid(v):
    return 0.5 * jnp.tanh(0.5 * v) + 0.5


def silu_pair(v):
    sig = sigmoid(v)
    value = v * sig
    return value, sig + value * (1.0 - sig)


def rows_to_eight(rows, first):
    place = iota((8, rows[0].shape[1]), 0)
    out = jnp.zeros((8, rows[0].shape[1]), F32)
    for step, row in enumerate(rows):
        out = jnp.where(place == first + step, row, out)
    return out


def slot_ids(dst_row):
    blocks = []
    for d in TABLE:
        if d["kind"] <= 2:
            place = iota((d["rows"], EDGES), 0) + (ATOMS + d["offset"])
            blocks.append(onehot(place == dst_row))
    corners = [d for d in TABLE if d["kind"] == 3]
    place = iota((8 * len(corners), EDGES), 0)
    inner = place % 8
    base = jnp.zeros_like(place)
    for step, d in enumerate(corners):
        base = jnp.where(place // 8 == step, ATOMS + d["offset"], base)
    blocks.append(onehot((inner < 4) & (base + inner == dst_row)))
    return jnp.concatenate(blocks, axis=0)


def edge_pass(pre_nodes, pos_i, pos_j, in_fill, same, w):
    diff = pos_j - pos_i
    qx, qy, qz = diff[4:5], diff[5:6], diff[6:7]
    live = pos_j[7:8]
    rsq = qx * qx + qy * qy + qz * qz
    in_use = in_fill * live
    inside = jnp.where(rsq < 1.0, 1.0 - rsq, 0.0)
    env = inside * inside * in_use
    centers = iota((8, EDGES), 0).astype(F32) / 7.0
    offset = rsq - centers
    radial = jnp.exp(-SHARPNESS * offset * offset)

    r3, r15, r5 = math.sqrt(3.0), math.sqrt(15.0), math.sqrt(5.0)
    y1 = rows_to_eight([r3 * qx, r3 * qy, r3 * qz], 0)
    y2 = rows_to_eight(
        [
            r15 * qx * qy,
            r15 * qy * qz,
            r15 * qz * qx,
            0.5 * r15 * (qx * qx - qy * qy),
            0.5 * r5 * (2.0 * qz * qz - qx * qx - qy * qy),
        ],
        0,
    )
    h1, l1 = (part.astype(F32) for part in split(y1, 2))
    h2, l2 = (part.astype(F32) for part in split(y2, 2))
    zero8 = jnp.zeros((8, EDGES), F32)
    left1 = jnp.concatenate([h1, h1, l1, zero8], axis=0).astype(BF16)
    right1 = jnp.concatenate([h1, l1, h1, zero8], axis=0).astype(BF16)
    left2 = jnp.concatenate([h2, h2, l2, zero8], axis=0).astype(BF16)
    right2 = jnp.concatenate([h2, l2, h2, zero8], axis=0).astype(BF16)
    k0 = same
    k1 = tn(left1, right1).astype(BF16) * same
    k2 = tn(left2, right2).astype(BF16) * same

    pre = pre_nodes + mm(w["rad_t"], radial.astype(BF16))
    act, dact = silu_pair(pre)
    latent = (act * env).astype(BF16)
    envw = mm(w["env_t"], latent).astype(BF16)
    scal0 = mm(envw, k0).astype(BF16)
    scal1 = mm(envw, k1).astype(BF16)
    scal2 = mm(envw, k2).astype(BF16)
    joined = jnp.concatenate([latent, scal0, scal1, scal2], axis=0)
    upd = mm(w["lat_t"], joined)
    upd_act, upd_d = silu_pair(upd)
    updated = (latent.astype(F32) + upd_act).astype(BF16)
    hid = mm(w["hid_t"], updated)
    hid_act, hid_d = silu_pair(hid)
    ro = w["ro"]
    denv = jnp.sum(hid_act * ro, axis=0, keepdims=True)
    dhid = (hid_d * ro * env).astype(BF16)
    dupdated = mm(w["hid"], dhid).astype(BF16).astype(F32)
    dupd = (dupdated * upd_d).astype(BF16)
    djoined = mm(w["lat"], dupd).astype(BF16)
    ds0 = djoined[CH : 2 * CH]
    ds1 = djoined[2 * CH : 3 * CH]
    ds2 = djoined[3 * CH :]
    denvw = (mm(ds0, k0) + mm(ds1, k1) + mm(ds2, k2)).astype(BF16)
    dlatent = dupdated + djoined[:CH].astype(F32) + mm(w["env"], denvw)
    dpre = (dlatent * env * dact).astype(BF16)
    denv = denv + jnp.sum(dlatent * act, axis=0, keepdims=True)

    envw_t = envw.T
    t1 = mm(jnp.concatenate([ds1.T, envw_t], axis=1), jnp.concatenate([envw, ds1], axis=0)).astype(BF16) * same
    t2 = mm(jnp.concatenate([ds2.T, envw_t], axis=1), jnp.concatenate([envw, ds2], axis=0)).astype(BF16) * same
    dy1 = mm(left1, t1)
    dy1 = dy1[0:8] + dy1[16:24]
    dy2 = mm(left2, t2)
    dy2 = dy2[0:8] + dy2[16:24]

    drad = mm(w["rad"], dpre)
    drsq = jnp.sum(drad * radial * offset, axis=0, keepdims=True) * (-2.0 * SHARPNESS)
    drsq = drsq - 2.0 * denv * in_use * inside
    a0, a1, a2, a3, a4 = (dy2[step : step + 1] for step in range(5))
    two = 2.0 * drsq
    gx = two * qx + r3 * dy1[0:1] + r15 * (a0 * qy + a2 * qz + a3 * qx) - r5 * a4 * qx
    gy = two * qy + r3 * dy1[1:2] + r15 * (a0 * qx + a1 * qz - a3 * qy) - r5 * a4 * qy
    gz = two * qz + r3 * dy1[2:3] + r15 * (a1 * qy + a2 * qx) + 2.0 * r5 * a4 * qz
    return dpre, rows_to_eight([gx, gy, gz], 4)


def kernel(
    prefix_hbm,
    fill_hbm,
    feat_hbm,
    pos_hbm,
    send_hbm,
    src_hbm,
    dst_hbm,
    wsrc_hbm,
    wdst_hbm,
    wrad_hbm,
    wenv_hbm,
    wlat_hbm,
    whid_hbm,
    wro_hbm,
    force_ref,
    grad_ref,
    prefix,
    fill,
    feat_v,
    pos_v,
    send_v,
    src_v,
    dst_v,
    wsrc_v,
    wdst_v,
    wrad_v,
    wenv_v,
    wlat_v,
    whid_v,
    wro_v,
    list_v,
    pick_v,
    out1,
    in1,
    out2,
    in2,
    in_sem,
    s1,
    r1,
    s2,
    r2,
):
    planes = lax.axis_size("dom") // ROW_Y
    depth = lax.axis_size("gz")
    dom = lax.axis_index("dom")
    cz = lax.axis_index("gz")
    cx, cy = dom // ROW_Y, dom % ROW_Y

    def place(vec, sign):
        x = (cx + sign * vec[0] + planes) % planes
        y = (cy + sign * vec[1] + ROW_Y) % ROW_Y
        z = (cz + sign * vec[2] + depth) % depth
        return (x * ROW_Y + y, z)

    loads = []
    for step, (source, target) in enumerate(
        [
            (send_hbm, send_v),
            (prefix_hbm, prefix),
            (feat_hbm, feat_v),
            (pos_hbm, pos_v),
            (src_hbm, src_v),
            (dst_hbm, dst_v),
            (wsrc_hbm, wsrc_v),
            (wdst_hbm, wdst_v),
            (wrad_hbm, wrad_v),
            (wenv_hbm, wenv_v),
            (wlat_hbm, wlat_v),
            (whid_hbm, whid_v),
            (wro_hbm, wro_v),
            (fill_hbm, fill),
        ]
    ):
        copy = pltpu.make_async_copy(source, target, in_sem.at[step])
        copy.start()
        loads.append(copy)

    barrier = pltpu.get_barrier_semaphore()
    for d in TABLE:
        pl.semaphore_signal(barrier, inc=1, device_id=place(d["vec"], 1), device_id_type=MESH)

    loads[0].wait()
    listed = jnp.where(iota((ATOMS, 608), 0) == send_v[...], 1.0, 0.0)
    list_v[0:608, :] = listed.T
    list_v[608:640, :] = jnp.zeros((32, ATOMS), F32)
    loads[1].wait()
    loads[2].wait()
    loads[3].wait()
    feat16 = feat_v[...].astype(BF16)
    pos = pos_v[...]
    own8 = rows_to_eight([pos[0:1], pos[1:2], pos[2:3], jnp.ones((1, ATOMS), F32)], 4)
    own_pieces = split_rows(own8, 3)
    lane = iota((8, 128), 1)
    line = iota((8, 128), 0)

    def store(ref, table, lines, slots, shifted):
        base = table[0]["slot"]
        for d in table:
            first = d["slot"] - base
            tile, low = first // 128 * 128, d["slot"] % 128
            inside = (lane >= low) & (lane < low + d["rows"]) & (line >= 4)
            coords = slots[:, tile : tile + 128]
            if shifted:
                shift = jnp.zeros((8, 128), F32)
                for step in range(3):
                    if d["vec"][step]:
                        shift = jnp.where(line == 4 + step, float(d["vec"][step]), shift)
                coords = coords - shift
            coords = jnp.where(inside, coords, 0.0)
            part = lines[first : first + d["rows"]]
            if d["kind"] == 3:
                ref[d["at"] : d["at"] + 8, :] = jnp.where(line < 4, part, coords)
            else:
                ref[d["at"] : d["at"] + d["rows"], :] = part
                ref[d["tile"] : d["tile"] + 8, :] = coords

    def send(table, source, target, send_sem, recv_sem, sign):
        for d in table:
            rows = pl.ds(d["at"], d["size"])
            pltpu.make_async_remote_copy(
                src_ref=source.at[rows],
                dst_ref=target.at[rows],
                send_sem=send_sem,
                recv_sem=recv_sem,
                device_id=place(d["vec"], sign),
                device_id_type=MESH,
            ).start()

    groups = [[d for d in TABLE if d["kind"] == 1], [d for d in TABLE if d["kind"] > 1]]
    picks = []
    for step, table in enumerate(groups):
        for d in table:
            n, rows = d["number"], d["rows"]
            count = prefix[0, n + 1] - prefix[0, n]
            lines = list_v[pl.ds(prefix[0, n], rows), :]
            pick_v[d["slot"] : d["slot"] + rows, :] = jnp.where(iota((rows, ATOMS), 0) < count, lines, 0.0)
        first, last = table[0]["slot"], table[-1]["slot"] + table[-1]["rows"]
        pick = pick_v[first:last, :].astype(BF16)
        picks.append(pick)
        store(out1, table, mm(pick, feat16), sum_pieces(nt(own_pieces, pick), 3), True)
        if step == 0:
            pl.semaphore_wait(barrier, len(TABLE))
        send(table, out1, in1, s1, r1, 1)
    pick = jnp.concatenate(picks, axis=0)

    for copy in loads[4:]:
        copy.wait()
    src_row, dst_row = src_v[...], dst_v[...]
    centre = onehot(iota((ATOMS, EDGES), 0) == src_row)
    near = onehot(iota((ATOMS, EDGES), 0) == dst_row)
    ghost = slot_ids(dst_row)
    same = (tn(centre, centre) * (1.0 / NEIGHBOURS)).astype(BF16)
    in_fill = jnp.where(iota((1, EDGES), 1) < fill[0], 1.0, 0.0)
    eye = iota((CH, CH), 0) == iota((CH, CH), 1)
    w = dict(
        dst_t=wdst_v[...].T,
        rad_t=wrad_v[...].T,
        env_t=wenv_v[...].T,
        lat_t=wlat_v[...].T,
        hid_t=whid_v[...].T,
        rad=wrad_v[...],
        env=wenv_v[...],
        lat=wlat_v[...],
        hid=whid_v[...],
        ro=jnp.sum(jnp.where(eye, wro_v[...], 0.0), axis=1, keepdims=True),
    )
    feat_t = feat16.T
    own_lhs = jnp.concatenate([feat_t, own_pieces], axis=0)
    at_i = mm(own_lhs, centre)
    at_j = mm(own_lhs, near)
    pre_own = mm(wsrc_v[...].T, at_i[:CH].astype(BF16)) + mm(w["dst_t"], at_j[:CH].astype(BF16))
    pos_i = sum_pieces(at_i[CH:], 3)
    pos_j_own = sum_pieces(at_j[CH:], 3)
    pick_t = pick.T

    def all_of(source, target, send_sem, recv_sem):
        return pltpu.make_async_remote_copy(
            src_ref=source,
            dst_ref=target,
            send_sem=send_sem,
            recv_sem=recv_sem,
            device_id=place(TABLE[0]["vec"], 1),
            device_id_type=MESH,
        )

    def unpack(ref):
        lines = jnp.concatenate([ref[d["at"] : d["at"] + d["rows"], :] for d in TABLE], axis=0)
        tiles = [None] * 5
        for d in TABLE:
            tile = d["slot"] // 128
            piece = ref[d["tile"] : d["tile"] + 8, :]
            tiles[tile] = piece if tiles[tile] is None else tiles[tile] + piece
        coords = jnp.concatenate(tiles, axis=1)
        coords = jnp.where(iota(coords.shape, 0) >= 4, coords, 0.0)
        return lines.astype(BF16), coords

    all_of(out1, in1, s1, r1).wait_recv()
    ghost_feat, ghost8 = unpack(in1)
    far = nt(w["dst_t"], ghost_feat).astype(BF16)
    arrived = mm(jnp.concatenate([far, split_rows(ghost8, 3)], axis=0), ghost)
    pos_j = pos_j_own + sum_pieces(arrived[CH:], 3)
    dpre, dq = edge_pass(pre_own + arrived[:CH], pos_i, pos_j, in_fill, same, w)

    dq_pieces = split_rows(dq, 2)
    for table in groups:
        first, last = table[0]["slot"], table[-1]["slot"] + table[-1]["rows"]
        hot = ghost[first:last]
        store(out2, table, nt(hot, dpre), sum_pieces(nt(dq_pieces, hot), 2), False)
        send(table, out2, in2, s2, r2, -1)

    own = nt(jnp.concatenate([centre, near], axis=0), dpre)
    own_src = nt(own[:ATOMS].astype(BF16), wsrc_v[...])
    own_dst = own[ATOMS:]
    own8 = sum_pieces(nt(dq_pieces, near - centre), 2)

    all_of(out2, in2, s2, r2).wait_recv()
    back_feat, back_pos = unpack(in2)
    sum_dst = own_dst + mm(pick_t, back_feat)
    grad_ref[...] = own_src + nt(sum_dst.astype(BF16), wdst_v[...])
    total8 = own8 + sum_pieces(mm(split_rows(back_pos, 2), pick), 2)
    force_ref[...] = -total8[4:7]
    all_of(out1, in1, s1, r1).wait_send()
    all_of(out2, in2, s2, r2).wait_send()


def pass_on(force_in, grad_in, force_out, grad_out, sems):
    copies = [
        pltpu.make_async_copy(force_in, force_out, sems.at[0]),
        pltpu.make_async_copy(grad_in, grad_out, sems.at[1]),
    ]
    for copy in copies:
        copy.start()
    for copy in copies:
        copy.wait()


def body(
    features,
    positions,
    send_ids,
    ghost_prefix,
    edge_fill,
    edge_src,
    edge_dst,
    weight_src,
    weight_dst,
    weight_radial,
    weight_env,
    weight_latent,
    weight_hidden,
    weight_readout,
):
    arrays = [
        features,
        positions,
        send_ids,
        edge_src,
        edge_dst,
        weight_src,
        weight_dst,
        weight_radial,
        weight_env,
        weight_latent,
        weight_hidden,
        weight_readout.reshape(1, CH),
    ]
    hbm = pl.BlockSpec(memory_space=pltpu.HBM)
    vmem = pl.BlockSpec(memory_space=pltpu.VMEM)
    results = (
        jax.ShapeDtypeStruct((3, ATOMS), F32),
        jax.ShapeDtypeStruct((ATOMS, CH), F32),
    )
    forces, feat_grad = pl.pallas_call(
        kernel,
        out_shape=results,
        in_specs=[hbm] * (2 + len(arrays)),
        out_specs=(vmem, vmem),
        scratch_shapes=[pltpu.SMEM(ghost_prefix.shape, jnp.int32), pltpu.SMEM(edge_fill.shape, jnp.int32)]
        + [pltpu.VMEM(a.shape, a.dtype) for a in arrays]
        + [
            pltpu.VMEM((SLOTS, ATOMS), F32),
            pltpu.VMEM((SLOTS, ATOMS), F32),
            pltpu.VMEM((PACK, CH), F32),
            pltpu.VMEM((PACK, CH), F32),
            pltpu.VMEM((PACK, CH), F32),
            pltpu.VMEM((PACK, CH), F32),
            pltpu.SemaphoreType.DMA((2 + len(arrays),)),
            pltpu.SemaphoreType.DMA,
            pltpu.SemaphoreType.DMA,
            pltpu.SemaphoreType.DMA,
            pltpu.SemaphoreType.DMA,
        ],
        compiler_params=pltpu.CompilerParams(
            collective_id=0, has_side_effects=True, vmem_limit_bytes=VMEM
        ),
        name="allegro",
    )(ghost_prefix, edge_fill, *arrays)
    return pl.pallas_call(
        pass_on,
        out_shape=results,
        in_specs=[hbm, hbm],
        out_specs=(hbm, hbm),
        scratch_shapes=[pltpu.SemaphoreType.DMA((2,))],
        compiler_params=pltpu.CompilerParams(vmem_limit_bytes=VMEM),
        name="pass_on",
    )(forces, feat_grad)


def solution(mesh):
    return jax.shard_map(
        body,
        mesh=mesh,
        in_specs=(
            P(("dom", "gz"), None),
            P(None, ("dom", "gz")),
            P(("dom", "gz"), None),
            P(("dom", "gz"), None),
            P(("dom", "gz")),
            P(("dom", "gz"), None),
            P(("dom", "gz"), None),
            P(),
            P(),
            P(),
            P(),
            P(),
            P(),
            P(),
        ),
        out_specs=(P(None, ("dom", "gz")), P(("dom", "gz"), None)),
        check_vma=False,
    )
```

time: 882 us -> 36.5 us (0.04); the launches traced: 869 us -> 36.4 us
  starting transfers between devices: 699 us -> 0 us
  other arithmetic: 73.6 us -> 0 us
  waiting for transfers between devices: 46.3 us -> 0 us
  local copies, waits for them, and re-layouts: 40.5 us -> 0 us
  Pallas kernels: 0 us -> 35.1 us
    ppermute x240 -> x0, starting transfers between devices: 699 us -> none  [shifted(): return lax.ppermute(value, axis, pairs)]
    ppermute x240 -> x0, waiting for transfers between devices: 46.3 us -> none  [shifted(): return lax.ppermute(value, axis, pairs)]
    scatter-add x8 -> x0, other arithmetic: 35.3 us -> none  [the longest x1 6.69 us: body(): jax.ops.segment_sum(back_feat * live_slot[:, None], owner_row, num_segmen...]
    pallas_call x0 -> x2, Pallas kernels: none -> 35.1 us  [the longest x1 32 us: body(): pl.pallas_call(kernel, out_shape=results, in_specs=[hbm] * (2 + len(array...]
    gather x20 -> x0, local copies, waits for them, and re-layouts: 29.2 us -> none  [the longest x2 4.95 us: local_energy(): gathered = environment[edge_source].reshape(edge_total, 9, channels)]
    concatenate x7 -> x0, other arithmetic: 17.4 us -> none  [the longest x1 17 us: body(): owner_row = send_ids[0, list_start]]
    convert_element_type x2 -> x0, other arithmetic: 17.2 us -> none  [the longest x1 17.1 us: body(): live_slot = (slot_index_arr < counts[slot_dir_arr]).astype(jnp.float32)]
  transfers between devices with their start and end apart: 240 -> 0, of which waited for: 33 -> 0; matrix products, arithmetic and copies ran while one was open for 2% -> 0% of each run, Pallas kernels for 0% -> 0%
where the time goes in v1:
time: 36.5 us; the launch traced here: 36.4 us
  Pallas kernels  35.1 us (96%)
  between operations  1.29 us (4%)
    pallas_call x1, Pallas kernels, body(): pl.pallas_call(kernel, out_shape=results, in_specs=[hbm] * (2 + len(array...  32 us
    pallas_call x1, Pallas kernels, body(): pl.pallas_call(pass_on, out_shape=results, in_specs=[hbm, hbm], out_specs...  3.15 us

profile of v1, /device:TPU:1, one launch (start us, length us, event | category | flops | bytes accessed | tf_op | source)
XLA Modules:
  0.0 36.4 jit_solution(879289267086316416)
XLA Ops:
  1.3 32.0 %allegro.1 = (f32[3,128]{1,0:T(4,128)}, f32[128,128]{1,0:T(8,128)}) custom-call(s32[1,27]{1,0:T(1,128)} %prefix_hbm.1, s32[1]{0:T(128)S(6)} %copy.16.fill_hbm, f32[128,128]{1,0:T(8,128)} %feat_hbm.1, f32[3,128]{1,0:T(4,128)} %pos_hbm.1, s32[1,608]{1,0:T(1,128)} %send_hbm.1, s32[1,512]{1,0:T(1,128)} %src_hbm.1, s32[1,512]{1,0:T(1,128)} %dst_hbm.1, ...), custom_call_target="tpu_custom_call" | custom-call | tf_op jit(solution)/shard_map/allegro/pallas_call | solution.py:495
  33.2 3.2 %pass_on.1 = (f32[3,128]{1,0:T(4,128)}, f32[128,128]{1,0:T(8,128)}) custom-call(f32[3,128]{1,0:T(4,128)} %get-tuple-element.4.force_in, f32[128,128]{1,0:T(8,128)} %get-tuple-element.5.grad_in), custom_call_target="tpu_custom_call" | custom-call | tf_op jit(solution)/shard_map/pass_on/pallas_call | solution.py:520

commit v2 on v1

--- a/solution.py
+++ b/solution.py
@@ -219,6 +219,18 @@
     return dpre, rows_to_eight([gx, gy, gz], 4)
 
 
+def unpack(ref):
+    lines = jnp.concatenate([ref[d["at"] : d["at"] + d["rows"], :] for d in TABLE], axis=0)
+    tiles = [None] * 5
+    for d in TABLE:
+        tile = d["slot"] // 128
+        piece = ref[d["tile"] : d["tile"] + 8, :]
+        tiles[tile] = piece if tiles[tile] is None else tiles[tile] + piece
+    coords = jnp.concatenate(tiles, axis=1)
+    coords = jnp.where(iota(coords.shape, 0) >= 4, coords, 0.0)
+    return lines.astype(BF16), coords
+
+
 def kernel(
     prefix_hbm,
     fill_hbm,
@@ -234,8 +246,9 @@
     wlat_hbm,
     whid_hbm,
     wro_hbm,
-    force_ref,
-    grad_ref,
+    in2,
+    own_hbm,
+    pick_hbm,
     prefix,
     fill,
     feat_v,
@@ -255,12 +268,14 @@
     out1,
     in1,
     out2,
-    in2,
+    own_v,
+    pick_t_v,
     in_sem,
     s1,
     r1,
     s2,
     r2,
+    out_sem,
 ):
     planes = lax.axis_size("dom") // ROW_Y
     depth = lax.axis_size("gz")
@@ -372,7 +387,7 @@
     near = onehot(iota((ATOMS, EDGES), 0) == dst_row)
     ghost = slot_ids(dst_row)
     same = (tn(centre, centre) * (1.0 / NEIGHBOURS)).astype(BF16)
-    in_fill = jnp.where(iota((1, EDGES), 1) < fill[0], 1.0, 0.0)
+    in_fill = jnp.where(iota((1, EDGES), 1) < fill[...], 1.0, 0.0)
     eye = iota((CH, CH), 0) == iota((CH, CH), 1)
     w = dict(
         dst_t=wdst_v[...].T,
@@ -393,7 +408,9 @@
     pre_own = mm(wsrc_v[...].T, at_i[:CH].astype(BF16)) + mm(w["dst_t"], at_j[:CH].astype(BF16))
     pos_i = sum_pieces(at_i[CH:], 3)
     pos_j_own = sum_pieces(at_j[CH:], 3)
-    pick_t = pick.T
+    pick_t_v[...] = pick.T
+    pick_out = pltpu.make_async_copy(pick_t_v, pick_hbm, out_sem.at[0])
+    pick_out.start()
 
     def all_of(source, target, send_sem, recv_sem):
         return pltpu.make_async_remote_copy(
@@ -405,17 +422,6 @@
             device_id_type=MESH,
         )
 
-    def unpack(ref):
-        lines = jnp.concatenate([ref[d["at"] : d["at"] + d["rows"], :] for d in TABLE], axis=0)
-        tiles = [None] * 5
-        for d in TABLE:
-            tile = d["slot"] // 128
-            piece = ref[d["tile"] : d["tile"] + 8, :]
-            tiles[tile] = piece if tiles[tile] is None else tiles[tile] + piece
-        coords = jnp.concatenate(tiles, axis=1)
-        coords = jnp.where(iota(coords.shape, 0) >= 4, coords, 0.0)
-        return lines.astype(BF16), coords
-
     all_of(out1, in1, s1, r1).wait_recv()
     ghost_feat, ghost8 = unpack(in1)
     far = nt(w["dst_t"], ghost_feat).astype(BF16)
@@ -430,30 +436,25 @@
         store(out2, table, nt(hot, dpre), sum_pieces(nt(dq_pieces, hot), 2), False)
         send(table, out2, in2, s2, r2, -1)
 
-    own = nt(jnp.concatenate([centre, near], axis=0), dpre)
-    own_src = nt(own[:ATOMS].astype(BF16), wsrc_v[...])
-    own_dst = own[ATOMS:]
-    own8 = sum_pieces(nt(dq_pieces, near - centre), 2)
-
-    all_of(out2, in2, s2, r2).wait_recv()
-    back_feat, back_pos = unpack(in2)
-    sum_dst = own_dst + mm(pick_t, back_feat)
-    grad_ref[...] = own_src + nt(sum_dst.astype(BF16), wdst_v[...])
-    total8 = own8 + sum_pieces(mm(split_rows(back_pos, 2), pick), 2)
+    own = nt(jnp.concatenate([centre, near], axis=0), dpre).astype(BF16)
+    own_v[0:ATOMS, :] = nt(own[:ATOMS], wsrc_v[...]) + nt(own[ATOMS:], wdst_v[...])
+    own_v[ATOMS:, :] = sum_pieces(nt(dq_pieces, near - centre), 2)
+    own_out = pltpu.make_async_copy(own_v, own_hbm, out_sem.at[1])
+    own_out.start()
+
+    pick_out.wait()
+    own_out.wait()
+    all_of(out1, in1, s1, r1).wait_send()
+    all_of(out2, in2, s2, r2).wait()
+
+
+def finish(back_ref, own_ref, pick_ref, wdst_ref, force_ref, grad_ref):
+    back_feat, back_pos = unpack(back_ref)
+    pick_t = pick_ref[...]
+    returned = mm(pick_t, back_feat).astype(BF16)
+    grad_ref[...] = own_ref[0:ATOMS, :] + nt(returned, wdst_ref[...])
+    total8 = own_ref[ATOMS:, :] + sum_pieces(nt(split_rows(back_pos, 2), pick_t), 2)
     force_ref[...] = -total8[4:7]
-    all_of(out1, in1, s1, r1).wait_send()
-    all_of(out2, in2, s2, r2).wait_send()
-
-
-def pass_on(force_in, grad_in, force_out, grad_out, sems):
-    copies = [
-        pltpu.make_async_copy(force_in, force_out, sems.at[0]),
-        pltpu.make_async_copy(grad_in, grad_out, sems.at[1]),
-    ]
-    for copy in copies:
-        copy.start()
-    for copy in copies:
-        copy.wait()
 
 
 def body(
@@ -488,16 +489,16 @@
     ]
     hbm = pl.BlockSpec(memory_space=pltpu.HBM)
     vmem = pl.BlockSpec(memory_space=pltpu.VMEM)
-    results = (
-        jax.ShapeDtypeStruct((3, ATOMS), F32),
-        jax.ShapeDtypeStruct((ATOMS, CH), F32),
-    )
-    forces, feat_grad = pl.pallas_call(
+    back, own, pick_t = pl.pallas_call(
         kernel,
-        out_shape=results,
+        out_shape=(
+            jax.ShapeDtypeStruct((PACK, CH), F32),
+            jax.ShapeDtypeStruct((ATOMS + 8, CH), F32),
+            jax.ShapeDtypeStruct((ATOMS, SLOTS), BF16),
+        ),
         in_specs=[hbm] * (2 + len(arrays)),
-        out_specs=(vmem, vmem),
-        scratch_shapes=[pltpu.SMEM(ghost_prefix.shape, jnp.int32), pltpu.SMEM(edge_fill.shape, jnp.int32)]
+        out_specs=(hbm, hbm, hbm),
+        scratch_shapes=[pltpu.SMEM(ghost_prefix.shape, jnp.int32), pltpu.VMEM((1, 1), jnp.int32)]
         + [pltpu.VMEM(a.shape, a.dtype) for a in arrays]
         + [
             pltpu.VMEM((SLOTS, ATOMS), F32),
@@ -505,27 +506,29 @@
             pltpu.VMEM((PACK, CH), F32),
             pltpu.VMEM((PACK, CH), F32),
             pltpu.VMEM((PACK, CH), F32),
-            pltpu.VMEM((PACK, CH), F32),
+            pltpu.VMEM((ATOMS + 8, CH), F32),
+            pltpu.VMEM((ATOMS, SLOTS), BF16),
             pltpu.SemaphoreType.DMA((2 + len(arrays),)),
             pltpu.SemaphoreType.DMA,
             pltpu.SemaphoreType.DMA,
             pltpu.SemaphoreType.DMA,
             pltpu.SemaphoreType.DMA,
+            pltpu.SemaphoreType.DMA((2,)),
         ],
-        compiler_params=pltpu.CompilerParams(
-            collective_id=0, has_side_effects=True, vmem_limit_bytes=VMEM
+        compiler_params=pltpu.CompilerParams(collective_id=0, has_side_effects=True, vmem_limit_bytes=VMEM),
+        name="allegro",
+    )(ghost_prefix, edge_fill.reshape(1, 1), *arrays)
+    return pl.pallas_call(
+        finish,
+        out_shape=(
+            jax.ShapeDtypeStruct((3, ATOMS), F32),
+            jax.ShapeDtypeStruct((ATOMS, CH), F32),
         ),
-        name="allegro",
-    )(ghost_prefix, edge_fill, *arrays)
-    return pl.pallas_call(
-        pass_on,
-        out_shape=results,
-        in_specs=[hbm, hbm],
-        out_specs=(hbm, hbm),
-        scratch_shapes=[pltpu.SemaphoreType.DMA((2,))],
+        in_specs=[vmem] * 4,
+        out_specs=(vmem, vmem),
         compiler_params=pltpu.CompilerParams(vmem_limit_bytes=VMEM),
-        name="pass_on",
-    )(forces, feat_grad)
+        name="finish",
+    )(back, own, pick_t, weight_dst)
 
 
 def solution(mesh):

time: 36.5 us -> 34.6 us (0.948)
  Pallas kernels: 35.1 us -> 33.1 us
    pallas_call x2, Pallas kernels: 35.1 us -> 33.1 us  [the longest x1 31.1 us: body(): pl.pallas_call(kernel, out_shape=(jax.ShapeDtypeStruct((PACK, CH), F32),...]
where the time goes in v2:
time: 34.6 us; the launch traced here: 34.4 us
  Pallas kernels  33.1 us (96%)
  between operations  1.29 us (4%)
    pallas_call x1, Pallas kernels, body(): pl.pallas_call(kernel, out_shape=(jax.ShapeDtypeStruct((PACK, CH), F32),...  31.1 us
    pallas_call x1, Pallas kernels, body(): pl.pallas_call(finish, out_shape=(jax.ShapeDtypeStruct((3, ATOMS), F32),...  2.03 us

profile of v2, /device:TPU:1, one launch (start us, length us, event | category | flops | bytes accessed | tf_op | source)
XLA Modules:
  0.0 34.4 jit_solution(11558172398710710161)
XLA Ops:
  1.3 31.1 %allegro.1 = (f32[784,128]{1,0:T(8,128)}, f32[136,128]{1,0:T(8,128)}, bf16[128,640]{1,0:T(8,128)(2,1)}) custom-call(s32[1,27]{1,0:T(1,128)} %prefix_hbm.1, s32[1,1]{1,0:T(1,128)} %bitcast.2.fill_hbm, f32[128,128]{1,0:T(8,128)} %feat_hbm.1, f32[3,128]{1,0:T(4,128)} %pos_hbm.1, s32[1,608]{1,0:T(1,128)} %send_hbm.1, s32[1,512]{1,0:T(1,128)} %src_hbm.1, ...), custom_call_target="tpu_custom_call" | custom-call | tf_op jit(solution)/shard_map/allegro/pallas_call | solution.py:492
  32.4 2.0 %finish.1 = (f32[3,128]{1,0:T(4,128)}, f32[128,128]{1,0:T(8,128)}) custom-call(f32[784,128]{1,0:T(8,128)} %get-tuple-element.5.back_ref, f32[136,128]{1,0:T(8,128)} %get-tuple-element.6.own_ref, bf16[128,640]{1,0:T(8,128)(2,1)} %get-tuple-element.7.pick_ref, bf16[128,128]{1,0:T(8,128)(2,1)} %wdst_ref.1), custom_call_target="tpu_custom_call" | custom-call | tf_op jit(solution)/shard_map/finish/pallas_call | solution.py:521

commit v3 on v2

--- a/solution.py
+++ b/solution.py
@@ -39,21 +39,20 @@
                 offset += cap
                 number += 1
     table.sort(key=lambda d: (d["kind"], d["number"]))
-    row = 0
     slot = 0
-    for d in table:
+    for step, d in enumerate(table):
         d["rows"] = {1: 64, 2: 16, 3: 8}[d["kind"]]
         d["slot"] = slot
-        d["at"] = row
-        d["size"] = {1: 72, 2: 24, 3: 8}[d["kind"]]
-        d["tile"] = row + {1: 64, 2: 16, 3: 0}[d["kind"]]
+        d["tile"] = 8 * step
         slot += d["rows"]
-        row += d["size"]
     assert slot == SLOTS
-    return table, row
-
-
-TABLE, PACK = directions()
+    return table
+
+
+TABLE = directions()
+FEAT_SENT = sum(d["cap"] for d in TABLE)
+COORDS = 8 * len(TABLE)
+COORDS_SENT = 4 * len(TABLE)
 
 
 def mm(a, b):
@@ -138,7 +137,7 @@
     return jnp.concatenate(blocks, axis=0)
 
 
-def edge_pass(pre_nodes, pos_i, pos_j, in_fill, same, w):
+def geometry(pos_i, pos_j, in_fill, same):
     diff = pos_j - pos_i
     qx, qy, qz = diff[4:5], diff[5:6], diff[6:7]
     live = pos_j[7:8]
@@ -169,11 +168,26 @@
     right1 = jnp.concatenate([h1, l1, h1, zero8], axis=0).astype(BF16)
     left2 = jnp.concatenate([h2, h2, l2, zero8], axis=0).astype(BF16)
     right2 = jnp.concatenate([h2, l2, h2, zero8], axis=0).astype(BF16)
-    k0 = same
     k1 = tn(left1, right1).astype(BF16) * same
     k2 = tn(left2, right2).astype(BF16) * same
 
-    pre = pre_nodes + mm(w["rad_t"], radial.astype(BF16))
+    return dict(
+        q=(qx, qy, qz),
+        in_use=in_use,
+        inside=inside,
+        env=env,
+        offset=offset,
+        radial=radial,
+        left1=left1,
+        left2=left2,
+        kernels=(same, k1, k2),
+    )
+
+
+def edge_pass(pre_nodes, geo, same, w):
+    env = geo["env"]
+    k0, k1, k2 = geo["kernels"]
+    pre = pre_nodes + mm(w["rad_t"], geo["radial"].astype(BF16))
     act, dact = silu_pair(pre)
     latent = (act * env).astype(BF16)
     envw = mm(w["env_t"], latent).astype(BF16)
@@ -198,37 +212,48 @@
     denvw = (mm(ds0, k0) + mm(ds1, k1) + mm(ds2, k2)).astype(BF16)
     dlatent = dupdated + djoined[:CH].astype(F32) + mm(w["env"], denvw)
     dpre = (dlatent * env * dact).astype(BF16)
+    return dpre, (dlatent, act, denv, envw, ds1, ds2)
+
+
+def edge_coords(dpre, kept, geo, same, w):
+    dlatent, act, denv, envw, ds1, ds2 = kept
+    r3, r15, r5 = math.sqrt(3.0), math.sqrt(15.0), math.sqrt(5.0)
+    qx, qy, qz = geo["q"]
     denv = denv + jnp.sum(dlatent * act, axis=0, keepdims=True)
-
     envw_t = envw.T
     t1 = mm(jnp.concatenate([ds1.T, envw_t], axis=1), jnp.concatenate([envw, ds1], axis=0)).astype(BF16) * same
     t2 = mm(jnp.concatenate([ds2.T, envw_t], axis=1), jnp.concatenate([envw, ds2], axis=0)).astype(BF16) * same
-    dy1 = mm(left1, t1)
+    dy1 = mm(geo["left1"], t1)
     dy1 = dy1[0:8] + dy1[16:24]
-    dy2 = mm(left2, t2)
+    dy2 = mm(geo["left2"], t2)
     dy2 = dy2[0:8] + dy2[16:24]
 
     drad = mm(w["rad"], dpre)
-    drsq = jnp.sum(drad * radial * offset, axis=0, keepdims=True) * (-2.0 * SHARPNESS)
-    drsq = drsq - 2.0 * denv * in_use * inside
+    drsq = jnp.sum(drad * geo["radial"] * geo["offset"], axis=0, keepdims=True) * (-2.0 * SHARPNESS)
+    drsq = drsq - 2.0 * denv * geo["in_use"] * geo["inside"]
     a0, a1, a2, a3, a4 = (dy2[step : step + 1] for step in range(5))
     two = 2.0 * drsq
     gx = two * qx + r3 * dy1[0:1] + r15 * (a0 * qy + a2 * qz + a3 * qx) - r5 * a4 * qx
     gy = two * qy + r3 * dy1[1:2] + r15 * (a0 * qx + a1 * qz - a3 * qy) - r5 * a4 * qy
     gz = two * qz + r3 * dy1[2:3] + r15 * (a1 * qy + a2 * qx) + 2.0 * r5 * a4 * qz
-    return dpre, rows_to_eight([gx, gy, gz], 4)
-
-
-def unpack(ref):
-    lines = jnp.concatenate([ref[d["at"] : d["at"] + d["rows"], :] for d in TABLE], axis=0)
-    tiles = [None] * 5
+    return rows_to_eight([gx, gy, gz], 4)
+
+
+def unpack_lines(ref):
+    first = [d for d in TABLE if d["kind"] == 3][0]["slot"]
+    corners = ref[first:, :]
+    corners = jnp.where(iota(corners.shape, 0) % 8 < 4, corners, 0.0)
+    return jnp.concatenate([ref[0:first, :], corners], axis=0).astype(BF16)
+
+
+def unpack_coords(ref):
+    tiles = [None] * (SLOTS // 128)
     for d in TABLE:
         tile = d["slot"] // 128
-        piece = ref[d["tile"] : d["tile"] + 8, :]
+        piece = ref[d["tile"] : d["tile"] + 4, :]
         tiles[tile] = piece if tiles[tile] is None else tiles[tile] + piece
     coords = jnp.concatenate(tiles, axis=1)
-    coords = jnp.where(iota(coords.shape, 0) >= 4, coords, 0.0)
-    return lines.astype(BF16), coords
+    return jnp.concatenate([jnp.zeros_like(coords), coords], axis=0)
 
 
 def kernel(
@@ -247,6 +272,7 @@
     whid_hbm,
     wro_hbm,
     in2,
+    coords_in2,
     own_hbm,
     pick_hbm,
     prefix,
@@ -267,14 +293,14 @@
     pick_v,
     out1,
     in1,
+    coords_out1,
+    coords_in1,
     out2,
+    coords_out2,
     own_v,
     pick_t_v,
     in_sem,
-    s1,
-    r1,
-    s2,
-    r2,
+    sems,
     out_sem,
 ):
     planes = lax.axis_size("dom") // ROW_Y
@@ -330,12 +356,10 @@
     lane = iota((8, 128), 1)
     line = iota((8, 128), 0)
 
-    def store(ref, table, lines, slots, shifted):
-        base = table[0]["slot"]
-        for d in table:
-            first = d["slot"] - base
-            tile, low = first // 128 * 128, d["slot"] % 128
-            inside = (lane >= low) & (lane < low + d["rows"]) & (line >= 4)
+    def store_coords(ref, slots, shifted):
+        for d in TABLE:
+            tile, low = d["slot"] // 128 * 128, d["slot"] % 128
+            inside = (lane >= low) & (lane < low + d["rows"])
             coords = slots[:, tile : tile + 128]
             if shifted:
                 shift = jnp.zeros((8, 128), F32)
@@ -343,42 +367,47 @@
                     if d["vec"][step]:
                         shift = jnp.where(line == 4 + step, float(d["vec"][step]), shift)
                 coords = coords - shift
-            coords = jnp.where(inside, coords, 0.0)
-            part = lines[first : first + d["rows"]]
-            if d["kind"] == 3:
-                ref[d["at"] : d["at"] + 8, :] = jnp.where(line < 4, part, coords)
-            else:
-                ref[d["at"] : d["at"] + d["rows"], :] = part
-                ref[d["tile"] : d["tile"] + 8, :] = coords
-
-    def send(table, source, target, send_sem, recv_sem, sign):
+            ref[d["tile"] : d["tile"] + 4, :] = jnp.where(inside, coords, 0.0)[4:8]
+
+    def remote(source, target, start, size, pair, vec, sign):
+        rows = pl.ds(start, size)
+        return pltpu.make_async_remote_copy(
+            src_ref=source.at[rows],
+            dst_ref=target.at[rows],
+            send_sem=sems.at[pair],
+            recv_sem=sems.at[pair + 1],
+            device_id=place(vec, sign),
+            device_id_type=MESH,
+        )
+
+    def send_lines(table, source, target, pair, sign):
         for d in table:
-            rows = pl.ds(d["at"], d["size"])
-            pltpu.make_async_remote_copy(
-                src_ref=source.at[rows],
-                dst_ref=target.at[rows],
-                send_sem=send_sem,
-                recv_sem=recv_sem,
-                device_id=place(d["vec"], sign),
-                device_id_type=MESH,
-            ).start()
-
+            remote(source, target, d["slot"], d["cap"], pair, d["vec"], sign).start()
+
+    def send_coords(source, target, pair, sign):
+        for d in TABLE:
+            remote(source, target, d["tile"], 4, pair, d["vec"], sign).start()
+
+    def lines_of(source, target, pair):
+        return remote(source, target, 0, FEAT_SENT, pair, TABLE[0]["vec"], 1)
+
+    def coords_of(source, target, pair):
+        return remote(source, target, 0, COORDS_SENT, pair, TABLE[0]["vec"], 1)
+
+    for d in TABLE:
+        n, rows = d["number"], d["rows"]
+        count = prefix[0, n + 1] - prefix[0, n]
+        lines = list_v[pl.ds(prefix[0, n], rows), :]
+        pick_v[d["slot"] : d["slot"] + rows, :] = jnp.where(iota((rows, ATOMS), 0) < count, lines, 0.0)
+    pick = pick_v[...].astype(BF16)
+    store_coords(coords_out1, sum_pieces(nt(own_pieces, pick), 3), True)
+    pl.semaphore_wait(barrier, len(TABLE))
+    send_coords(coords_out1, coords_in1, 0, 1)
     groups = [[d for d in TABLE if d["kind"] == 1], [d for d in TABLE if d["kind"] > 1]]
-    picks = []
-    for step, table in enumerate(groups):
-        for d in table:
-            n, rows = d["number"], d["rows"]
-            count = prefix[0, n + 1] - prefix[0, n]
-            lines = list_v[pl.ds(prefix[0, n], rows), :]
-            pick_v[d["slot"] : d["slot"] + rows, :] = jnp.where(iota((rows, ATOMS), 0) < count, lines, 0.0)
-        first, last = table[0]["slot"], table[-1]["slot"] + table[-1]["rows"]
-        pick = pick_v[first:last, :].astype(BF16)
-        picks.append(pick)
-        store(out1, table, mm(pick, feat16), sum_pieces(nt(own_pieces, pick), 3), True)
-        if step == 0:
-            pl.semaphore_wait(barrier, len(TABLE))
-        send(table, out1, in1, s1, r1, 1)
-    pick = jnp.concatenate(picks, axis=0)
+    spans = [(table[0]["slot"], table[-1]["slot"] + table[-1]["rows"]) for table in groups]
+    for table, (first, last) in zip(groups, spans):
+        out1[first:last, :] = mm(pick[first:last], feat16)
+        send_lines(table, out1, in1, 2, 1)
 
     for copy in loads[4:]:
         copy.wait()
@@ -412,29 +441,20 @@
     pick_out = pltpu.make_async_copy(pick_t_v, pick_hbm, out_sem.at[0])
     pick_out.start()
 
-    def all_of(source, target, send_sem, recv_sem):
-        return pltpu.make_async_remote_copy(
-            src_ref=source,
-            dst_ref=target,
-            send_sem=send_sem,
-            recv_sem=recv_sem,
-            device_id=place(TABLE[0]["vec"], 1),
-            device_id_type=MESH,
-        )
-
-    all_of(out1, in1, s1, r1).wait_recv()
-    ghost_feat, ghost8 = unpack(in1)
-    far = nt(w["dst_t"], ghost_feat).astype(BF16)
-    arrived = mm(jnp.concatenate([far, split_rows(ghost8, 3)], axis=0), ghost)
-    pos_j = pos_j_own + sum_pieces(arrived[CH:], 3)
-    dpre, dq = edge_pass(pre_own + arrived[:CH], pos_i, pos_j, in_fill, same, w)
-
-    dq_pieces = split_rows(dq, 2)
-    for table in groups:
-        first, last = table[0]["slot"], table[-1]["slot"] + table[-1]["rows"]
-        hot = ghost[first:last]
-        store(out2, table, nt(hot, dpre), sum_pieces(nt(dq_pieces, hot), 2), False)
-        send(table, out2, in2, s2, r2, -1)
+    coords_of(coords_out1, coords_in1, 0).wait_recv()
+    pos_g = mm(split_rows(unpack_coords(coords_in1), 3), ghost)
+    geo = geometry(pos_i, pos_j_own + sum_pieces(pos_g, 3), in_fill, same)
+
+    lines_of(out1, in1, 2).wait_recv()
+    far = nt(w["dst_t"], unpack_lines(in1)).astype(BF16)
+    dpre, kept = edge_pass(pre_own + mm(far, ghost), geo, same, w)
+
+    for table, (first, last) in zip(groups, spans):
+        out2[first:last, :] = nt(ghost[first:last], dpre)
+        send_lines(table, out2, in2, 4, -1)
+    dq_pieces = split_rows(edge_coords(dpre, kept, geo, same, w), 2)
+    store_coords(coords_out2, sum_pieces(nt(dq_pieces, ghost), 2), False)
+    send_coords(coords_out2, coords_in2, 6, -1)
 
     own = nt(jnp.concatenate([centre, near], axis=0), dpre).astype(BF16)
     own_v[0:ATOMS, :] = nt(own[:ATOMS], wsrc_v[...]) + nt(own[ATOMS:], wdst_v[...])
@@ -444,16 +464,17 @@
 
     pick_out.wait()
     own_out.wait()
-    all_of(out1, in1, s1, r1).wait_send()
-    all_of(out2, in2, s2, r2).wait()
-
-
-def finish(back_ref, own_ref, pick_ref, wdst_ref, force_ref, grad_ref):
-    back_feat, back_pos = unpack(back_ref)
+    coords_of(coords_out1, coords_in1, 0).wait_send()
+    lines_of(out1, in1, 2).wait_send()
+    lines_of(out2, in2, 4).wait()
+    coords_of(coords_out2, coords_in2, 6).wait()
+
+
+def finish(back_ref, coords_ref, own_ref, pick_ref, wdst_ref, force_ref, grad_ref):
     pick_t = pick_ref[...]
-    returned = mm(pick_t, back_feat).astype(BF16)
+    returned = mm(pick_t, unpack_lines(back_ref)).astype(BF16)
     grad_ref[...] = own_ref[0:ATOMS, :] + nt(returned, wdst_ref[...])
-    total8 = own_ref[ATOMS:, :] + sum_pieces(nt(split_rows(back_pos, 2), pick_t), 2)
+    total8 = own_ref[ATOMS:, :] + sum_pieces(nt(split_rows(unpack_coords(coords_ref), 2), pick_t), 2)
     force_ref[...] = -total8[4:7]
 
 
@@ -489,30 +510,31 @@
     ]
     hbm = pl.BlockSpec(memory_space=pltpu.HBM)
     vmem = pl.BlockSpec(memory_space=pltpu.VMEM)
-    back, own, pick_t = pl.pallas_call(
+    back, coords, own, pick_t = pl.pallas_call(
         kernel,
         out_shape=(
-            jax.ShapeDtypeStruct((PACK, CH), F32),
+            jax.ShapeDtypeStruct((SLOTS, CH), F32),
+            jax.ShapeDtypeStruct((COORDS, CH), F32),
             jax.ShapeDtypeStruct((ATOMS + 8, CH), F32),
             jax.ShapeDtypeStruct((ATOMS, SLOTS), BF16),
         ),
         in_specs=[hbm] * (2 + len(arrays)),
-        out_specs=(hbm, hbm, hbm),
+        out_specs=(hbm, hbm, hbm, hbm),
         scratch_shapes=[pltpu.SMEM(ghost_prefix.shape, jnp.int32), pltpu.VMEM((1, 1), jnp.int32)]
         + [pltpu.VMEM(a.shape, a.dtype) for a in arrays]
         + [
             pltpu.VMEM((SLOTS, ATOMS), F32),
             pltpu.VMEM((SLOTS, ATOMS), F32),
-            pltpu.VMEM((PACK, CH), F32),
-            pltpu.VMEM((PACK, CH), F32),
-            pltpu.VMEM((PACK, CH), F32),
+            pltpu.VMEM((SLOTS, CH), F32),
+            pltpu.VMEM((SLOTS, CH), F32),
+            pltpu.VMEM((COORDS, CH), F32),
+            pltpu.VMEM((COORDS, CH), F32),
+            pltpu.VMEM((SLOTS, CH), F32),
+            pltpu.VMEM((COORDS, CH), F32),
             pltpu.VMEM((ATOMS + 8, CH), F32),
             pltpu.VMEM((ATOMS, SLOTS), BF16),
             pltpu.SemaphoreType.DMA((2 + len(arrays),)),
-            pltpu.SemaphoreType.DMA,
-            pltpu.SemaphoreType.DMA,
-            pltpu.SemaphoreType.DMA,
-            pltpu.SemaphoreType.DMA,
+            pltpu.SemaphoreType.DMA((8,)),
             pltpu.SemaphoreType.DMA((2,)),
         ],
         compiler_params=pltpu.CompilerParams(collective_id=0, has_side_effects=True, vmem_limit_bytes=VMEM),
@@ -524,11 +546,11 @@
             jax.ShapeDtypeStruct((3, ATOMS), F32),
             jax.ShapeDtypeStruct((ATOMS, CH), F32),
         ),
-        in_specs=[vmem] * 4,
+        in_specs=[vmem] * 5,
         out_specs=(vmem, vmem),
         compiler_params=pltpu.CompilerParams(vmem_limit_bytes=VMEM),
         name="finish",
-    )(back, own, pick_t, weight_dst)
+    )(back, coords, own, pick_t, weight_dst)
 
 
 def solution(mesh):

time: 34.6 us -> 33.5 us (0.968)
  Pallas kernels: 33.1 us -> 32.1 us
    pallas_call x1, Pallas kernels: 31.1 us -> 30 us  [body(): pl.pallas_call(kernel, out_shape=(jax.ShapeDtypeStruct((SLOTS, CH), F32),...]
where the time goes in v3:
time: 33.5 us; the launch traced here: 33.4 us
  Pallas kernels  32.1 us (96%)
  between operations  1.29 us (4%)
    pallas_call x1, Pallas kernels, body(): pl.pallas_call(kernel, out_shape=(jax.ShapeDtypeStruct((SLOTS, CH), F32),...  30 us
    pallas_call x1, Pallas kernels, body(): pl.pallas_call(finish, out_shape=(jax.ShapeDtypeStruct((3, ATOMS), F32),...  2.08 us

profile of v3, /device:TPU:1, one launch (start us, length us, event | category | flops | bytes accessed | tf_op | source)
XLA Modules:
  0.0 33.4 jit_solution(15558494790411586544)
XLA Ops:
  1.3 30.0 %allegro.1 = (f32[640,128]{1,0:T(8,128)}, f32[208,128]{1,0:T(8,128)}, f32[136,128]{1,0:T(8,128)}, bf16[128,640]{1,0:T(8,128)(2,1)}) custom-call(s32[1,27]{1,0:T(1,128)} %prefix_hbm.1, s32[1,1]{1,0:T(1,128)} %bitcast.2.fill_hbm, f32[128,128]{1,0:T(8,128)} %feat_hbm.1, f32[3,128]{1,0:T(4,128)} %pos_hbm.1, s32[1,608]{1,0:T(1,128)} %send_hbm.1, ...), custom_call_target="tpu_custom_call" | custom-call | tf_op jit(solution)/shard_map/allegro/pallas_call | solution.py:513
  31.3 2.1 %finish.1 = (f32[3,128]{1,0:T(4,128)}, f32[128,128]{1,0:T(8,128)}) custom-call(f32[640,128]{1,0:T(8,128)} %get-tuple-element.6.back_ref, f32[208,128]{1,0:T(8,128)} %get-tuple-element.7.coords_ref, f32[136,128]{1,0:T(8,128)} %get-tuple-element.8.own_ref, bf16[128,640]{1,0:T(8,128)(2,1)} %get-tuple-element.9.pick_ref, bf16[128,128]{1,0:T(8,128)(2,1)} %wdst_ref.1), custom_call_target="tpu_custom_call" | custom-call | tf_op jit(solution)/shard_map/finish/pallas_call | solution.py:543

commit v4 on v3

--- a/solution.py
+++ b/solution.py
@@ -307,13 +307,13 @@
     depth = lax.axis_size("gz")
     dom = lax.axis_index("dom")
     cz = lax.axis_index("gz")
-    cx, cy = dom // ROW_Y, dom % ROW_Y
+    cx, cy = lax.div(dom, ROW_Y), lax.rem(dom, ROW_Y)
+    along_x = {step: lax.rem(cx + (step + planes), planes) * ROW_Y for step in (-1, 0, 1)}
+    along_y = {step: lax.rem(cy + (step + ROW_Y), ROW_Y) for step in (-1, 0, 1)}
+    along_z = {step: lax.rem(cz + (step + depth), depth) for step in (-1, 0, 1)}
 
     def place(vec, sign):
-        x = (cx + sign * vec[0] + planes) % planes
-        y = (cy + sign * vec[1] + ROW_Y) % ROW_Y
-        z = (cz + sign * vec[2] + depth) % depth
-        return (x * ROW_Y + y, z)
+        return (along_x[sign * vec[0]] + along_y[sign * vec[1]], along_z[sign * vec[2]])
 
     loads = []
     for step, (source, target) in enumerate(
@@ -385,7 +385,7 @@
             remote(source, target, d["slot"], d["cap"], pair, d["vec"], sign).start()
 
     def send_coords(source, target, pair, sign):
-        for d in TABLE:
+        for d in TABLE[::-1]:
             remote(source, target, d["tile"], 4, pair, d["vec"], sign).start()
 
     def lines_of(source, target, pair):
@@ -401,12 +401,13 @@
         pick_v[d["slot"] : d["slot"] + rows, :] = jnp.where(iota((rows, ATOMS), 0) < count, lines, 0.0)
     pick = pick_v[...].astype(BF16)
     store_coords(coords_out1, sum_pieces(nt(own_pieces, pick), 3), True)
+    out1[...] = mm(pick, feat16)
+    groups = [[d for d in TABLE[::-1] if d["kind"] > 1], [d for d in TABLE if d["kind"] == 1]]
+    split_at = groups[1][-1]["slot"] + groups[1][-1]["rows"]
+    spans = [(split_at, SLOTS), (0, split_at)]
     pl.semaphore_wait(barrier, len(TABLE))
     send_coords(coords_out1, coords_in1, 0, 1)
-    groups = [[d for d in TABLE if d["kind"] == 1], [d for d in TABLE if d["kind"] > 1]]
-    spans = [(table[0]["slot"], table[-1]["slot"] + table[-1]["rows"]) for table in groups]
-    for table, (first, last) in zip(groups, spans):
-        out1[first:last, :] = mm(pick[first:last], feat16)
+    for table in groups:
         send_lines(table, out1, in1, 2, 1)
 
     for copy in loads[4:]:

time: 33.5 us -> 32.6 us (0.973)
  Pallas kernels: 32.1 us -> 31.1 us
    pallas_call x1, Pallas kernels: 30 us -> 29 us  [body(): pl.pallas_call(kernel, out_shape=(jax.ShapeDtypeStruct((SLOTS, CH), F32),...]
where the time goes in v4:
time: 32.6 us; the launch traced here: 32.4 us
  Pallas kernels  31.1 us (95%)
  between operations  1.29 us (4%)
    pallas_call x1, Pallas kernels, body(): pl.pallas_call(kernel, out_shape=(jax.ShapeDtypeStruct((SLOTS, CH), F32),...  29 us
    pallas_call x1, Pallas kernels, body(): pl.pallas_call(finish, out_shape=(jax.ShapeDtypeStruct((3, ATOMS), F32),...  2.08 us

profile of v4, /device:TPU:1, one launch (start us, length us, event | category | flops | bytes accessed | tf_op | source)
XLA Modules:
  0.0 32.4 jit_solution(5420273355189033962)
XLA Ops:
  1.3 29.0 %allegro.1 = (f32[640,128]{1,0:T(8,128)}, f32[208,128]{1,0:T(8,128)}, f32[136,128]{1,0:T(8,128)}, bf16[128,640]{1,0:T(8,128)(2,1)}) custom-call(s32[1,27]{1,0:T(1,128)} %prefix_hbm.1, s32[1,1]{1,0:T(1,128)} %bitcast.2.fill_hbm, f32[128,128]{1,0:T(8,128)} %feat_hbm.1, f32[3,128]{1,0:T(4,128)} %pos_hbm.1, s32[1,608]{1,0:T(1,128)} %send_hbm.1, ...), custom_call_target="tpu_custom_call" | custom-call | tf_op jit(solution)/shard_map/allegro/pallas_call | solution.py:514
  30.3 2.1 %finish.1 = (f32[3,128]{1,0:T(4,128)}, f32[128,128]{1,0:T(8,128)}) custom-call(f32[640,128]{1,0:T(8,128)} %get-tuple-element.6.back_ref, f32[208,128]{1,0:T(8,128)} %get-tuple-element.7.coords_ref, f32[136,128]{1,0:T(8,128)} %get-tuple-element.8.own_ref, bf16[128,640]{1,0:T(8,128)(2,1)} %get-tuple-element.9.pick_ref, bf16[128,128]{1,0:T(8,128)(2,1)} %wdst_ref.1), custom_call_target="tpu_custom_call" | custom-call | tf_op jit(solution)/shard_map/finish/pallas_call | solution.py:544

commit v5 on v4

--- a/solution.py
+++ b/solution.py
@@ -137,6 +137,18 @@
     return jnp.concatenate(blocks, axis=0)
 
 
+def side_by_side(x):
+    rows = x.shape[0] // 3
+    return jnp.concatenate([x[rows * step : rows * (step + 1)] for step in range(3)], axis=1)
+
+
+def mixing(wenv, wlat):
+    parts = [wlat[:CH]]
+    for step in range(1, 4):
+        parts.append(mm(wenv, wlat[CH * step : CH * (step + 1)]).astype(BF16))
+    return parts
+
+
 def geometry(pos_i, pos_j, in_fill, same):
     diff = pos_j - pos_i
     qx, qy, qz = diff[4:5], diff[5:6], diff[6:7]
@@ -180,49 +192,39 @@
         radial=radial,
         left1=left1,
         left2=left2,
-        kernels=(same, k1, k2),
+        kernels=jnp.concatenate([same, k1, k2], axis=0),
     )
 
 
-def edge_pass(pre_nodes, geo, same, w):
-    env = geo["env"]
-    k0, k1, k2 = geo["kernels"]
-    pre = pre_nodes + mm(w["rad_t"], geo["radial"].astype(BF16))
+def edge_pass(pre, geo, w):
+    env, kernels = geo["env"], geo["kernels"]
     act, dact = silu_pair(pre)
     latent = (act * env).astype(BF16)
-    envw = mm(w["env_t"], latent).astype(BF16)
-    scal0 = mm(envw, k0).astype(BF16)
-    scal1 = mm(envw, k1).astype(BF16)
-    scal2 = mm(envw, k2).astype(BF16)
-    joined = jnp.concatenate([latent, scal0, scal1, scal2], axis=0)
-    upd = mm(w["lat_t"], joined)
+    mixed = mm(w["mix_t"], latent)
+    near_far = mixed[CH:].astype(BF16)
+    upd = mixed[:CH] + mm(side_by_side(near_far), kernels)
     upd_act, upd_d = silu_pair(upd)
     updated = (latent.astype(F32) + upd_act).astype(BF16)
     hid = mm(w["hid_t"], updated)
     hid_act, hid_d = silu_pair(hid)
     ro = w["ro"]
-    denv = jnp.sum(hid_act * ro, axis=0, keepdims=True)
     dhid = (hid_d * ro * env).astype(BF16)
     dupdated = mm(w["hid"], dhid).astype(BF16).astype(F32)
     dupd = (dupdated * upd_d).astype(BF16)
-    djoined = mm(w["lat"], dupd).astype(BF16)
-    ds0 = djoined[CH : 2 * CH]
-    ds1 = djoined[2 * CH : 3 * CH]
-    ds2 = djoined[3 * CH :]
-    denvw = (mm(ds0, k0) + mm(ds1, k1) + mm(ds2, k2)).astype(BF16)
-    dlatent = dupdated + djoined[:CH].astype(F32) + mm(w["env"], denvw)
+    dmixed = mm(w["mix"], dupd)
+    dlatent = dupdated + dmixed[:CH] + mm(side_by_side(dmixed[CH:].astype(BF16)), kernels)
     dpre = (dlatent * env * dact).astype(BF16)
-    return dpre, (dlatent, act, denv, envw, ds1, ds2)
+    return dpre, (dlatent, act, hid_act, near_far[CH : 2 * CH], near_far[2 * CH :], dupd)
 
 
 def edge_coords(dpre, kept, geo, same, w):
-    dlatent, act, denv, envw, ds1, ds2 = kept
+    dlatent, act, hid_act, b1, b2, dupd = kept
     r3, r15, r5 = math.sqrt(3.0), math.sqrt(15.0), math.sqrt(5.0)
     qx, qy, qz = geo["q"]
-    denv = denv + jnp.sum(dlatent * act, axis=0, keepdims=True)
-    envw_t = envw.T
-    t1 = mm(jnp.concatenate([ds1.T, envw_t], axis=1), jnp.concatenate([envw, ds1], axis=0)).astype(BF16) * same
-    t2 = mm(jnp.concatenate([ds2.T, envw_t], axis=1), jnp.concatenate([envw, ds2], axis=0)).astype(BF16) * same
+    denv = jnp.sum(hid_act * w["ro"] + dlatent * act, axis=0, keepdims=True)
+    dupd_t = dupd.T
+    t1 = mm(jnp.concatenate([dupd_t, b1.T], axis=1), jnp.concatenate([b1, dupd], axis=0)).astype(BF16) * same
+    t2 = mm(jnp.concatenate([dupd_t, b2.T], axis=1), jnp.concatenate([b2, dupd], axis=0)).astype(BF16) * same
     dy1 = mm(geo["left1"], t1)
     dy1 = dy1[0:8] + dy1[16:24]
     dy2 = mm(geo["left2"], t2)
@@ -419,15 +421,14 @@
     same = (tn(centre, centre) * (1.0 / NEIGHBOURS)).astype(BF16)
     in_fill = jnp.where(iota((1, EDGES), 1) < fill[...], 1.0, 0.0)
     eye = iota((CH, CH), 0) == iota((CH, CH), 1)
+    mix = mixing(wenv_v[...], wlat_v[...])
     w = dict(
         dst_t=wdst_v[...].T,
         rad_t=wrad_v[...].T,
-        env_t=wenv_v[...].T,
-        lat_t=wlat_v[...].T,
+        mix=jnp.concatenate(mix, axis=0),
+        mix_t=jnp.concatenate([part.T for part in mix], axis=0),
         hid_t=whid_v[...].T,
         rad=wrad_v[...],
-        env=wenv_v[...],
-        lat=wlat_v[...],
         hid=whid_v[...],
         ro=jnp.sum(jnp.where(eye, wro_v[...], 0.0), axis=1, keepdims=True),
     )
@@ -446,9 +447,11 @@
     pos_g = mm(split_rows(unpack_coords(coords_in1), 3), ghost)
     geo = geometry(pos_i, pos_j_own + sum_pieces(pos_g, 3), in_fill, same)
 
+    pre_known = pre_own + mm(w["rad_t"], geo["radial"].astype(BF16))
+
     lines_of(out1, in1, 2).wait_recv()
     far = nt(w["dst_t"], unpack_lines(in1)).astype(BF16)
-    dpre, kept = edge_pass(pre_own + mm(far, ghost), geo, same, w)
+    dpre, kept = edge_pass(pre_known + mm(far, ghost), geo, w)
 
     for table, (first, last) in zip(groups, spans):
         out2[first:last, :] = nt(ghost[first:last], dpre)

time: 32.6 us -> 32.2 us (0.988)
    pallas_call x1, Pallas kernels: 29 us -> 28.7 us  [body(): pl.pallas_call(kernel, out_shape=(jax.ShapeDtypeStruct((SLOTS, CH), F32),...]
where the time goes in v5:
time: 32.2 us; the launch traced here: 32.1 us
  Pallas kernels  30.8 us (96%)
  between operations  1.29 us (4%)
    pallas_call x1, Pallas kernels, body(): pl.pallas_call(kernel, out_shape=(jax.ShapeDtypeStruct((SLOTS, CH), F32),...  28.7 us
    pallas_call x1, Pallas kernels, body(): pl.pallas_call(finish, out_shape=(jax.ShapeDtypeStruct((3, ATOMS), F32),...  2.08 us

profile of v5, /device:TPU:1, one launch (start us, length us, event | category | flops | bytes accessed | tf_op | source)
XLA Modules:
  0.0 32.1 jit_solution(18357312012078950415)
XLA Ops:
  1.3 28.7 %allegro.1 = (f32[640,128]{1,0:T(8,128)}, f32[208,128]{1,0:T(8,128)}, f32[136,128]{1,0:T(8,128)}, bf16[128,640]{1,0:T(8,128)(2,1)}) custom-call(s32[1,27]{1,0:T(1,128)} %prefix_hbm.1, s32[1,1]{1,0:T(1,128)} %bitcast.2.fill_hbm, f32[128,128]{1,0:T(8,128)} %feat_hbm.1, f32[3,128]{1,0:T(4,128)} %pos_hbm.1, s32[1,608]{1,0:T(1,128)} %send_hbm.1, ...), custom_call_target="tpu_custom_call" | custom-call | tf_op jit(solution)/shard_map/allegro/pallas_call | solution.py:517
  30.0 2.1 %finish.1 = (f32[3,128]{1,0:T(4,128)}, f32[128,128]{1,0:T(8,128)}) custom-call(f32[640,128]{1,0:T(8,128)} %get-tuple-element.6.back_ref, f32[208,128]{1,0:T(8,128)} %get-tuple-element.7.coords_ref, f32[136,128]{1,0:T(8,128)} %get-tuple-element.8.own_ref, bf16[128,640]{1,0:T(8,128)(2,1)} %get-tuple-element.9.pick_ref, bf16[128,128]{1,0:T(8,128)(2,1)} %wdst_ref.1), custom_call_target="tpu_custom_call" | custom-call | tf_op jit(solution)/shard_map/finish/pallas_call | solution.py:547

commit v6 on v5

--- a/solution.py
+++ b/solution.py
@@ -50,9 +50,12 @@
 
 
 TABLE = directions()
-FEAT_SENT = sum(d["cap"] for d in TABLE)
+FACES = [d for d in TABLE if d["kind"] == 1]
+LINES = [d for d in TABLE if d["kind"] == 2]
+CORNERS = [d for d in TABLE if d["kind"] == 3]
+LINES_AT, CORNERS_AT = LINES[0]["slot"], CORNERS[0]["slot"]
 COORDS = 8 * len(TABLE)
-COORDS_SENT = 4 * len(TABLE)
+COORDS_SENT = 4 * len(TABLE) + 4 * len(CORNERS)
 
 
 def mm(a, b):
@@ -127,13 +130,12 @@
         if d["kind"] <= 2:
             place = iota((d["rows"], EDGES), 0) + (ATOMS + d["offset"])
             blocks.append(onehot(place == dst_row))
-    corners = [d for d in TABLE if d["kind"] == 3]
-    place = iota((8 * len(corners), EDGES), 0)
+    place = iota((8 * len(CORNERS), EDGES), 0)
     inner = place % 8
     base = jnp.zeros_like(place)
-    for step, d in enumerate(corners):
-        base = jnp.where(place // 8 == step, ATOMS + d["offset"], base)
-    blocks.append(onehot((inner < 4) & (base + inner == dst_row)))
+    for step, d in enumerate(CORNERS):
+        base = jnp.where(place // 8 == step, ATOMS - 4 + d["offset"], base)
+    blocks.append(onehot((inner >= 4) & (base + inner == dst_row)))
     return jnp.concatenate(blocks, axis=0)
 
 
@@ -214,17 +216,20 @@
     dmixed = mm(w["mix"], dupd)
     dlatent = dupdated + dmixed[:CH] + mm(side_by_side(dmixed[CH:].astype(BF16)), kernels)
     dpre = (dlatent * env * dact).astype(BF16)
-    return dpre, (dlatent, act, hid_act, near_far[CH : 2 * CH], near_far[2 * CH :], dupd)
+    b1, b2 = near_far[CH : 2 * CH], near_far[2 * CH :]
+    dupd_t = dupd.T
+    pairs = [
+        (jnp.concatenate([dupd_t, b.T], axis=1), jnp.concatenate([b, dupd], axis=0)) for b in (b1, b2)
+    ]
+    return dpre, (dlatent, act, hid_act, pairs)
 
 
 def edge_coords(dpre, kept, geo, same, w):
-    dlatent, act, hid_act, b1, b2, dupd = kept
+    dlatent, act, hid_act, pairs = kept
     r3, r15, r5 = math.sqrt(3.0), math.sqrt(15.0), math.sqrt(5.0)
     qx, qy, qz = geo["q"]
     denv = jnp.sum(hid_act * w["ro"] + dlatent * act, axis=0, keepdims=True)
-    dupd_t = dupd.T
-    t1 = mm(jnp.concatenate([dupd_t, b1.T], axis=1), jnp.concatenate([b1, dupd], axis=0)).astype(BF16) * same
-    t2 = mm(jnp.concatenate([dupd_t, b2.T], axis=1), jnp.concatenate([b2, dupd], axis=0)).astype(BF16) * same
+    t1, t2 = (mm(*pair).astype(BF16) * same for pair in pairs)
     dy1 = mm(geo["left1"], t1)
     dy1 = dy1[0:8] + dy1[16:24]
     dy2 = mm(geo["left2"], t2)
@@ -241,11 +246,9 @@
     return rows_to_eight([gx, gy, gz], 4)
 
 
-def unpack_lines(ref):
-    first = [d for d in TABLE if d["kind"] == 3][0]["slot"]
-    corners = ref[first:, :]
-    corners = jnp.where(iota(corners.shape, 0) % 8 < 4, corners, 0.0)
-    return jnp.concatenate([ref[0:first, :], corners], axis=0).astype(BF16)
+def corner_lines(ref):
+    tiles = ref[CORNERS[0]["tile"] :, :]
+    return jnp.where(iota(tiles.shape, 0) % 8 >= 4, tiles, 0.0).astype(BF16)
 
 
 def unpack_coords(ref):
@@ -358,7 +361,7 @@
     lane = iota((8, 128), 1)
     line = iota((8, 128), 0)
 
-    def store_coords(ref, slots, shifted):
+    def store_coords(ref, slots, corners, shifted):
         for d in TABLE:
             tile, low = d["slot"] // 128 * 128, d["slot"] % 128
             inside = (lane >= low) & (lane < low + d["rows"])
@@ -369,7 +372,11 @@
                     if d["vec"][step]:
                         shift = jnp.where(line == 4 + step, float(d["vec"][step]), shift)
                 coords = coords - shift
-            ref[d["tile"] : d["tile"] + 4, :] = jnp.where(inside, coords, 0.0)[4:8]
+            coords = jnp.where(inside, coords, 0.0)[4:8]
+            if d["kind"] == 3:
+                first = d["slot"] - CORNERS_AT
+                coords = jnp.concatenate([coords, corners[first + 4 : first + 8]], axis=0)
+            ref[d["tile"] : d["tile"] + coords.shape[0], :] = coords
 
     def remote(source, target, start, size, pair, vec, sign):
         rows = pl.ds(start, size)
@@ -384,14 +391,14 @@
 
     def send_lines(table, source, target, pair, sign):
         for d in table:
-            remote(source, target, d["slot"], d["cap"], pair, d["vec"], sign).start()
+            remote(source, target, d["slot"], d["rows"], pair, d["vec"], sign).start()
 
     def send_coords(source, target, pair, sign):
         for d in TABLE[::-1]:
-            remote(source, target, d["tile"], 4, pair, d["vec"], sign).start()
-
-    def lines_of(source, target, pair):
-        return remote(source, target, 0, FEAT_SENT, pair, TABLE[0]["vec"], 1)
+            remote(source, target, d["tile"], 8 if d["kind"] == 3 else 4, pair, d["vec"], sign).start()
+
+    def lines_of(source, target, pair, first, last):
+        return remote(source, target, first, last - first, pair, TABLE[0]["vec"], 1)
 
     def coords_of(source, target, pair):
         return remote(source, target, 0, COORDS_SENT, pair, TABLE[0]["vec"], 1)
@@ -400,17 +407,18 @@
         n, rows = d["number"], d["rows"]
         count = prefix[0, n + 1] - prefix[0, n]
         lines = list_v[pl.ds(prefix[0, n], rows), :]
-        pick_v[d["slot"] : d["slot"] + rows, :] = jnp.where(iota((rows, ATOMS), 0) < count, lines, 0.0)
+        lines = jnp.where(iota((rows, ATOMS), 0) < count, lines, 0.0)
+        if d["kind"] == 3:
+            lines = jnp.concatenate([jnp.zeros((4, ATOMS), F32), lines[:4]], axis=0)
+        pick_v[d["slot"] : d["slot"] + rows, :] = lines
     pick = pick_v[...].astype(BF16)
-    store_coords(coords_out1, sum_pieces(nt(own_pieces, pick), 3), True)
-    out1[...] = mm(pick, feat16)
-    groups = [[d for d in TABLE[::-1] if d["kind"] > 1], [d for d in TABLE if d["kind"] == 1]]
-    split_at = groups[1][-1]["slot"] + groups[1][-1]["rows"]
-    spans = [(split_at, SLOTS), (0, split_at)]
+    packed = mm(pick, feat16)
+    store_coords(coords_out1, sum_pieces(nt(own_pieces, pick), 3), packed[CORNERS_AT:], True)
+    out1[...] = packed[:CORNERS_AT]
     pl.semaphore_wait(barrier, len(TABLE))
     send_coords(coords_out1, coords_in1, 0, 1)
-    for table in groups:
-        send_lines(table, out1, in1, 2, 1)
+    send_lines(LINES, out1, in1, 2, 1)
+    send_lines(FACES, out1, in1, 4, 1)
 
     for copy in loads[4:]:
         copy.wait()
@@ -449,16 +457,21 @@
 
     pre_known = pre_own + mm(w["rad_t"], geo["radial"].astype(BF16))
 
-    lines_of(out1, in1, 2).wait_recv()
-    far = nt(w["dst_t"], unpack_lines(in1)).astype(BF16)
-    dpre, kept = edge_pass(pre_known + mm(far, ghost), geo, w)
-
-    for table, (first, last) in zip(groups, spans):
-        out2[first:last, :] = nt(ghost[first:last], dpre)
-        send_lines(table, out2, in2, 4, -1)
+    lines_of(out1, in1, 2, LINES_AT, CORNERS_AT).wait_recv()
+    some = jnp.concatenate([in1[LINES_AT:, :].astype(BF16), corner_lines(coords_in1)], axis=0)
+    pre_known = pre_known + mm(nt(w["dst_t"], some).astype(BF16), ghost[LINES_AT:])
+    lines_of(out1, in1, 4, 0, LINES_AT).wait_recv()
+    far = nt(w["dst_t"], in1[0:LINES_AT, :].astype(BF16)).astype(BF16)
+    dpre, kept = edge_pass(pre_known + mm(far, ghost[:LINES_AT]), geo, w)
+
+    some = nt(ghost[LINES_AT:], dpre)
+    out2[LINES_AT:, :] = some[: CORNERS_AT - LINES_AT]
+    send_lines(LINES, out2, in2, 6, -1)
+    out2[0:LINES_AT, :] = nt(ghost[:LINES_AT], dpre)
+    send_lines(FACES, out2, in2, 8, -1)
     dq_pieces = split_rows(edge_coords(dpre, kept, geo, same, w), 2)
-    store_coords(coords_out2, sum_pieces(nt(dq_pieces, ghost), 2), False)
-    send_coords(coords_out2, coords_in2, 6, -1)
+    store_coords(coords_out2, sum_pieces(nt(dq_pieces, ghost), 2), some[CORNERS_AT - LINES_AT :], False)
+    send_coords(coords_out2, coords_in2, 10, -1)
 
     own = nt(jnp.concatenate([centre, near], axis=0), dpre).astype(BF16)
     own_v[0:ATOMS, :] = nt(own[:ATOMS], wsrc_v[...]) + nt(own[ATOMS:], wdst_v[...])
@@ -469,14 +482,16 @@
     pick_out.wait()
     own_out.wait()
     coords_of(coords_out1, coords_in1, 0).wait_send()
-    lines_of(out1, in1, 2).wait_send()
-    lines_of(out2, in2, 4).wait()
-    coords_of(coords_out2, coords_in2, 6).wait()
+    for pair, first, last in ((2, LINES_AT, CORNERS_AT), (4, 0, LINES_AT)):
+        lines_of(out1, in1, pair, first, last).wait_send()
+        lines_of(out2, in2, pair + 4, first, last).wait()
+    coords_of(coords_out2, coords_in2, 10).wait()
 
 
 def finish(back_ref, coords_ref, own_ref, pick_ref, wdst_ref, force_ref, grad_ref):
     pick_t = pick_ref[...]
-    returned = mm(pick_t, unpack_lines(back_ref)).astype(BF16)
+    lines = jnp.concatenate([back_ref[...].astype(BF16), corner_lines(coords_ref)], axis=0)
+    returned = mm(pick_t, lines).astype(BF16)
     grad_ref[...] = own_ref[0:ATOMS, :] + nt(returned, wdst_ref[...])
     total8 = own_ref[ATOMS:, :] + sum_pieces(nt(split_rows(unpack_coords(coords_ref), 2), pick_t), 2)
     force_ref[...] = -total8[4:7]
@@ -517,7 +532,7 @@
     back, coords, own, pick_t = pl.pallas_call(
         kernel,
         out_shape=(
-            jax.ShapeDtypeStruct((SLOTS, CH), F32),
+            jax.ShapeDtypeStruct((CORNERS_AT, CH), F32),
             jax.ShapeDtypeStruct((COORDS, CH), F32),
             jax.ShapeDtypeStruct((ATOMS + 8, CH), F32),
             jax.ShapeDtypeStruct((ATOMS, SLOTS), BF16),
@@ -529,16 +544,16 @@
         + [
             pltpu.VMEM((SLOTS, ATOMS), F32),
             pltpu.VMEM((SLOTS, ATOMS), F32),
-            pltpu.VMEM((SLOTS, CH), F32),
-            pltpu.VMEM((SLOTS, CH), F32),
+            pltpu.VMEM((CORNERS_AT, CH), F32),
+            pltpu.VMEM((CORNERS_AT, CH), F32),
             pltpu.VMEM((COORDS, CH), F32),
             pltpu.VMEM((COORDS, CH), F32),
-            pltpu.VMEM((SLOTS, CH), F32),
+            pltpu.VMEM((CORNERS_AT, CH), F32),
             pltpu.VMEM((COORDS, CH), F32),
             pltpu.VMEM((ATOMS + 8, CH), F32),
             pltpu.VMEM((ATOMS, SLOTS), BF16),
             pltpu.SemaphoreType.DMA((2 + len(arrays),)),
-            pltpu.SemaphoreType.DMA((8,)),
+            pltpu.SemaphoreType.DMA((12,)),
             pltpu.SemaphoreType.DMA((2,)),
         ],
         compiler_params=pltpu.CompilerParams(collective_id=0, has_side_effects=True, vmem_limit_bytes=VMEM),

time: 32.2 us -> 32.5 us (level)
    pallas_call x1, Pallas kernels: 28.7 us -> 29 us  [body(): pl.pallas_call(kernel, out_shape=(jax.ShapeDtypeStruct((CORNERS_AT, CH),...]
where the time goes in v6:
time: 32.5 us; the launch traced here: 32.4 us
  Pallas kernels  31.1 us (96%)
  between operations  1.29 us (4%)
    pallas_call x1, Pallas kernels, body(): pl.pallas_call(kernel, out_shape=(jax.ShapeDtypeStruct((CORNERS_AT, CH),...  29 us
    pallas_call x1, Pallas kernels, body(): pl.pallas_call(finish, out_shape=(jax.ShapeDtypeStruct((3, ATOMS), F32),...  2.07 us

profile of v6, /device:TPU:1, one launch (start us, length us, event | category | flops | bytes accessed | tf_op | source)
XLA Modules:
  0.0 32.4 jit_solution(110311232509088686)
XLA Ops:
  1.3 29.0 %allegro.1 = (f32[576,128]{1,0:T(8,128)}, f32[208,128]{1,0:T(8,128)}, f32[136,128]{1,0:T(8,128)}, bf16[128,640]{1,0:T(8,128)(2,1)}) custom-call(s32[1,27]{1,0:T(1,128)} %prefix_hbm.1, s32[1,1]{1,0:T(1,128)} %bitcast.2.fill_hbm, f32[128,128]{1,0:T(8,128)} %feat_hbm.1, f32[3,128]{1,0:T(4,128)} %pos_hbm.1, s32[1,608]{1,0:T(1,128)} %send_hbm.1, ...), custom_call_target="tpu_custom_call" | custom-call | tf_op jit(solution)/shard_map/allegro/pallas_call | solution.py:532
  30.3 2.1 %finish.1 = (f32[3,128]{1,0:T(4,128)}, f32[128,128]{1,0:T(8,128)}) custom-call(f32[576,128]{1,0:T(8,128)} %get-tuple-element.6.back_ref, f32[208,128]{1,0:T(8,128)} %get-tuple-element.7.coords_ref, f32[136,128]{1,0:T(8,128)} %get-tuple-element.8.own_ref, bf16[128,640]{1,0:T(8,128)(2,1)} %get-tuple-element.9.pick_ref, bf16[128,128]{1,0:T(8,128)(2,1)} %wdst_ref.1), custom_call_target="tpu_custom_call" | custom-call | tf_op jit(solution)/shard_map/finish/pallas_call | solution.py:562

commit v7 on v6

--- a/solution.py
+++ b/solution.py
@@ -111,9 +111,10 @@
 
 
 def silu_pair(v):
+    v = v.astype(BF16)
     sig = sigmoid(v)
     value = v * sig
-    return value, sig + value * (1.0 - sig)
+    return value, sig + value * (1 - sig)
 
 
 def rows_to_eight(rows, first):
@@ -200,22 +201,19 @@
 
 def edge_pass(pre, geo, w):
     env, kernels = geo["env"], geo["kernels"]
+    env16 = env.astype(BF16)
     act, dact = silu_pair(pre)
-    latent = (act * env).astype(BF16)
+    latent = act * env16
     mixed = mm(w["mix_t"], latent)
     near_far = mixed[CH:].astype(BF16)
-    upd = mixed[:CH] + mm(side_by_side(near_far), kernels)
-    upd_act, upd_d = silu_pair(upd)
-    updated = (latent.astype(F32) + upd_act).astype(BF16)
-    hid = mm(w["hid_t"], updated)
-    hid_act, hid_d = silu_pair(hid)
-    ro = w["ro"]
-    dhid = (hid_d * ro * env).astype(BF16)
-    dupdated = mm(w["hid"], dhid).astype(BF16).astype(F32)
-    dupd = (dupdated * upd_d).astype(BF16)
+    upd_act, upd_d = silu_pair(mixed[:CH] + mm(side_by_side(near_far), kernels))
+    hid_act, hid_d = silu_pair(mm(w["hid_t"], latent + upd_act))
+    dhid = hid_d * (w["ro"] * env).astype(BF16)
+    dupdated = mm(w["hid"], dhid)
+    dupd = dupdated.astype(BF16) * upd_d
     dmixed = mm(w["mix"], dupd)
     dlatent = dupdated + dmixed[:CH] + mm(side_by_side(dmixed[CH:].astype(BF16)), kernels)
-    dpre = (dlatent * env * dact).astype(BF16)
+    dpre = (dlatent * env).astype(BF16) * dact
     b1, b2 = near_far[CH : 2 * CH], near_far[2 * CH :]
     dupd_t = dupd.T
     pairs = [

time: 32.5 us -> 32.4 us (level)
  no operation moved by 1% of the time
where the time goes in v7:
time: 32.4 us; the launch traced here: 32.3 us
  Pallas kernels  31 us (96%)
  between operations  1.29 us (4%)
    pallas_call x1, Pallas kernels, body(): pl.pallas_call(kernel, out_shape=(jax.ShapeDtypeStruct((CORNERS_AT, CH),...  28.9 us
    pallas_call x1, Pallas kernels, body(): pl.pallas_call(finish, out_shape=(jax.ShapeDtypeStruct((3, ATOMS), F32),...  2.07 us

profile of v7, /device:TPU:1, one launch (start us, length us, event | category | flops | bytes accessed | tf_op | source)
XLA Modules:
  0.0 32.3 jit_solution(1071945584384016921)
XLA Ops:
  1.3 28.9 %allegro.1 = (f32[576,128]{1,0:T(8,128)}, f32[208,128]{1,0:T(8,128)}, f32[136,128]{1,0:T(8,128)}, bf16[128,640]{1,0:T(8,128)(2,1)}) custom-call(s32[1,27]{1,0:T(1,128)} %prefix_hbm.1, s32[1,1]{1,0:T(1,128)} %bitcast.2.fill_hbm, f32[128,128]{1,0:T(8,128)} %feat_hbm.1, f32[3,128]{1,0:T(4,128)} %pos_hbm.1, s32[1,608]{1,0:T(1,128)} %send_hbm.1, ...), custom_call_target="tpu_custom_call" | custom-call | tf_op jit(solution)/shard_map/allegro/pallas_call | solution.py:530
  30.2 2.1 %finish.1 = (f32[3,128]{1,0:T(4,128)}, f32[128,128]{1,0:T(8,128)}) custom-call(f32[576,128]{1,0:T(8,128)} %get-tuple-element.6.back_ref, f32[208,128]{1,0:T(8,128)} %get-tuple-element.7.coords_ref, f32[136,128]{1,0:T(8,128)} %get-tuple-element.8.own_ref, bf16[128,640]{1,0:T(8,128)(2,1)} %get-tuple-element.9.pick_ref, bf16[128,128]{1,0:T(8,128)(2,1)} %wdst_ref.1), custom_call_target="tpu_custom_call" | custom-call | tf_op jit(solution)/shard_map/finish/pallas_call | solution.py:560

commit v8 on v7

--- a/solution.py
+++ b/solution.py
@@ -220,6 +220,21 @@
         (jnp.concatenate([dupd_t, b.T], axis=1), jnp.concatenate([b, dupd], axis=0)) for b in (b1, b2)
     ]
     return dpre, (dlatent, act, hid_act, pairs)
+
+
+def slot_ids_across(dst_row):
+    dst = jnp.broadcast_to(dst_row.astype(F32), (128, EDGES)).T
+    blocks = []
+    for tile in range(SLOTS // 128):
+        lane = iota((8, 128), 1)
+        ids = jnp.full((8, 128), -1, jnp.int32)
+        for d in TABLE:
+            if d["slot"] // 128 == tile:
+                low = d["slot"] % 128 + (4 if d["kind"] == 3 else 0)
+                mine = (lane >= low) & (lane < low + d["cap"])
+                ids = jnp.where(mine, lane + (ATOMS + d["offset"] - low), ids)
+        blocks.append(onehot(dst == ids.astype(F32)[0:1]))
+    return jnp.concatenate(blocks, axis=1)
 
 
 def edge_coords(dpre, kept, geo, same, w):
@@ -424,6 +439,7 @@
     centre = onehot(iota((ATOMS, EDGES), 0) == src_row)
     near = onehot(iota((ATOMS, EDGES), 0) == dst_row)
     ghost = slot_ids(dst_row)
+    ghost_t = slot_ids_across(dst_row)
     same = (tn(centre, centre) * (1.0 / NEIGHBOURS)).astype(BF16)
     in_fill = jnp.where(iota((1, EDGES), 1) < fill[...], 1.0, 0.0)
     eye = iota((CH, CH), 0) == iota((CH, CH), 1)
@@ -468,7 +484,7 @@
     out2[0:LINES_AT, :] = nt(ghost[:LINES_AT], dpre)
     send_lines(FACES, out2, in2, 8, -1)
     dq_pieces = split_rows(edge_coords(dpre, kept, geo, same, w), 2)
-    store_coords(coords_out2, sum_pieces(nt(dq_pieces, ghost), 2), some[CORNERS_AT - LINES_AT :], False)
+    store_coords(coords_out2, sum_pieces(mm(dq_pieces, ghost_t), 2), some[CORNERS_AT - LINES_AT :], False)
     send_coords(coords_out2, coords_in2, 10, -1)
 
     own = nt(jnp.concatenate([centre, near], axis=0), dpre).astype(BF16)

time: 32.4 us -> 32.4 us (level)
  no operation moved by 1% of the time
where the time goes in v8:
time: 32.4 us; the launch traced here: 32.3 us
  Pallas kernels  31 us (96%)
  between operations  1.29 us (4%)
    pallas_call x1, Pallas kernels, body(): pl.pallas_call(kernel, out_shape=(jax.ShapeDtypeStruct((CORNERS_AT, CH),...  28.9 us
    pallas_call x1, Pallas kernels, body(): pl.pallas_call(finish, out_shape=(jax.ShapeDtypeStruct((3, ATOMS), F32),...  2.07 us

profile of v8, /device:TPU:1, one launch (start us, length us, event | category | flops | bytes accessed | tf_op | source)
XLA Modules:
  0.0 32.3 jit_solution(5875881417065778829)
XLA Ops:
  1.3 28.9 %allegro.1 = (f32[576,128]{1,0:T(8,128)}, f32[208,128]{1,0:T(8,128)}, f32[136,128]{1,0:T(8,128)}, bf16[128,640]{1,0:T(8,128)(2,1)}) custom-call(s32[1,27]{1,0:T(1,128)} %prefix_hbm.1, s32[1,1]{1,0:T(1,128)} %bitcast.2.fill_hbm, f32[128,128]{1,0:T(8,128)} %feat_hbm.1, f32[3,128]{1,0:T(4,128)} %pos_hbm.1, s32[1,608]{1,0:T(1,128)} %send_hbm.1, ...), custom_call_target="tpu_custom_call" | custom-call | tf_op jit(solution)/shard_map/allegro/pallas_call | solution.py:546
  30.2 2.1 %finish.1 = (f32[3,128]{1,0:T(4,128)}, f32[128,128]{1,0:T(8,128)}) custom-call(f32[576,128]{1,0:T(8,128)} %get-tuple-element.6.back_ref, f32[208,128]{1,0:T(8,128)} %get-tuple-element.7.coords_ref, f32[136,128]{1,0:T(8,128)} %get-tuple-element.8.own_ref, bf16[128,640]{1,0:T(8,128)(2,1)} %get-tuple-element.9.pick_ref, bf16[128,128]{1,0:T(8,128)(2,1)} %wdst_ref.1), custom_call_target="tpu_custom_call" | custom-call | tf_op jit(solution)/shard_map/finish/pallas_call | solution.py:576

commit v9 on v8

--- a/solution.py
+++ b/solution.py
@@ -53,6 +53,7 @@
 FACES = [d for d in TABLE if d["kind"] == 1]
 LINES = [d for d in TABLE if d["kind"] == 2]
 CORNERS = [d for d in TABLE if d["kind"] == 3]
+ORDER = sorted(TABLE, key=lambda d: (-d["kind"], d["vec"][2] == 0))
 LINES_AT, CORNERS_AT = LINES[0]["slot"], CORNERS[0]["slot"]
 COORDS = 8 * len(TABLE)
 COORDS_SENT = 4 * len(TABLE) + 4 * len(CORNERS)
@@ -353,12 +354,15 @@
         ]
     ):
         copy = pltpu.make_async_copy(source, target, in_sem.at[step])
+        loads.append(copy)
+
+    barrier = pltpu.get_barrier_semaphore()
+    for copy in loads[:4]:
         copy.start()
-        loads.append(copy)
-
-    barrier = pltpu.get_barrier_semaphore()
-    for d in TABLE:
+    for d in ORDER:
         pl.semaphore_signal(barrier, inc=1, device_id=place(d["vec"], 1), device_id_type=MESH)
+    for copy in loads[4:]:
+        copy.start()
 
     loads[0].wait()
     listed = jnp.where(iota((ATOMS, 608), 0) == send_v[...], 1.0, 0.0)
@@ -403,11 +407,13 @@
         )
 
     def send_lines(table, source, target, pair, sign):
-        for d in table:
+        for d in ORDER:
+            if d not in table:
+                continue
             remote(source, target, d["slot"], d["rows"], pair, d["vec"], sign).start()
 
     def send_coords(source, target, pair, sign):
-        for d in TABLE[::-1]:
+        for d in ORDER:
             remote(source, target, d["tile"], 8 if d["kind"] == 3 else 4, pair, d["vec"], sign).start()
 
     def lines_of(source, target, pair, first, last):

time: 32.4 us -> 32.1 us (level)
  no operation moved by 1% of the time
where the time goes in v9:
time: 32.1 us; the launch traced here: 32 us
  Pallas kernels  30.7 us (96%)
  between operations  1.29 us (4%)
    pallas_call x1, Pallas kernels, body(): pl.pallas_call(kernel, out_shape=(jax.ShapeDtypeStruct((CORNERS_AT, CH),...  28.6 us
    pallas_call x1, Pallas kernels, body(): pl.pallas_call(finish, out_shape=(jax.ShapeDtypeStruct((3, ATOMS), F32),...  2.07 us

profile of v9, /device:TPU:1, one launch (start us, length us, event | category | flops | bytes accessed | tf_op | source)
XLA Modules:
  0.0 32.0 jit_solution(7448992628255941714)
XLA Ops:
  1.3 28.6 %allegro.1 = (f32[576,128]{1,0:T(8,128)}, f32[208,128]{1,0:T(8,128)}, f32[136,128]{1,0:T(8,128)}, bf16[128,640]{1,0:T(8,128)(2,1)}) custom-call(s32[1,27]{1,0:T(1,128)} %prefix_hbm.1, s32[1,1]{1,0:T(1,128)} %bitcast.2.fill_hbm, f32[128,128]{1,0:T(8,128)} %feat_hbm.1, f32[3,128]{1,0:T(4,128)} %pos_hbm.1, s32[1,608]{1,0:T(1,128)} %send_hbm.1, ...), custom_call_target="tpu_custom_call" | custom-call | tf_op jit(solution)/shard_map/allegro/pallas_call | solution.py:552
  29.9 2.1 %finish.1 = (f32[3,128]{1,0:T(4,128)}, f32[128,128]{1,0:T(8,128)}) custom-call(f32[576,128]{1,0:T(8,128)} %get-tuple-element.6.back_ref, f32[208,128]{1,0:T(8,128)} %get-tuple-element.7.coords_ref, f32[136,128]{1,0:T(8,128)} %get-tuple-element.8.own_ref, bf16[128,640]{1,0:T(8,128)(2,1)} %get-tuple-element.9.pick_ref, bf16[128,128]{1,0:T(8,128)(2,1)} %wdst_ref.1), custom_call_target="tpu_custom_call" | custom-call | tf_op jit(solution)/shard_map/finish/pallas_call | solution.py:582

commit v10 on v9

--- a/solution.py
+++ b/solution.py
@@ -200,7 +200,7 @@
     )
 
 
-def edge_pass(pre, geo, w):
+def edge_pass(pre, geo, same, w):
     env, kernels = geo["env"], geo["kernels"]
     env16 = env.astype(BF16)
     act, dact = silu_pair(pre)
@@ -212,14 +212,14 @@
     dhid = hid_d * (w["ro"] * env).astype(BF16)
     dupdated = mm(w["hid"], dhid)
     dupd = dupdated.astype(BF16) * upd_d
+    dupd_t = dupd.T
+    pairs = [
+        mm(jnp.concatenate([dupd_t, b.T], axis=1), jnp.concatenate([b, dupd], axis=0)).astype(BF16) * same
+        for b in (near_far[CH : 2 * CH], near_far[2 * CH :])
+    ]
     dmixed = mm(w["mix"], dupd)
     dlatent = dupdated + dmixed[:CH] + mm(side_by_side(dmixed[CH:].astype(BF16)), kernels)
     dpre = (dlatent * env).astype(BF16) * dact
-    b1, b2 = near_far[CH : 2 * CH], near_far[2 * CH :]
-    dupd_t = dupd.T
-    pairs = [
-        (jnp.concatenate([dupd_t, b.T], axis=1), jnp.concatenate([b, dupd], axis=0)) for b in (b1, b2)
-    ]
     return dpre, (dlatent, act, hid_act, pairs)
 
 
@@ -238,12 +238,12 @@
     return jnp.concatenate(blocks, axis=1)
 
 
-def edge_coords(dpre, kept, geo, same, w):
+def edge_coords(dpre, kept, geo, w):
     dlatent, act, hid_act, pairs = kept
     r3, r15, r5 = math.sqrt(3.0), math.sqrt(15.0), math.sqrt(5.0)
     qx, qy, qz = geo["q"]
     denv = jnp.sum(hid_act * w["ro"] + dlatent * act, axis=0, keepdims=True)
-    t1, t2 = (mm(*pair).astype(BF16) * same for pair in pairs)
+    t1, t2 = pairs
     dy1 = mm(geo["left1"], t1)
     dy1 = dy1[0:8] + dy1[16:24]
     dy2 = mm(geo["left2"], t2)
@@ -482,14 +482,14 @@
     pre_known = pre_known + mm(nt(w["dst_t"], some).astype(BF16), ghost[LINES_AT:])
     lines_of(out1, in1, 4, 0, LINES_AT).wait_recv()
     far = nt(w["dst_t"], in1[0:LINES_AT, :].astype(BF16)).astype(BF16)
-    dpre, kept = edge_pass(pre_known + mm(far, ghost[:LINES_AT]), geo, w)
+    dpre, kept = edge_pass(pre_known + mm(far, ghost[:LINES_AT]), geo, same, w)
 
     some = nt(ghost[LINES_AT:], dpre)
     out2[LINES_AT:, :] = some[: CORNERS_AT - LINES_AT]
     send_lines(LINES, out2, in2, 6, -1)
     out2[0:LINES_AT, :] = nt(ghost[:LINES_AT], dpre)
     send_lines(FACES, out2, in2, 8, -1)
-    dq_pieces = split_rows(edge_coords(dpre, kept, geo, same, w), 2)
+    dq_pieces = split_rows(edge_coords(dpre, kept, geo, w), 2)
     store_coords(coords_out2, sum_pieces(mm(dq_pieces, ghost_t), 2), some[CORNERS_AT - LINES_AT :], False)
     send_coords(coords_out2, coords_in2, 10, -1)
 
@@ -508,13 +508,42 @@
     coords_of(coords_out2, coords_in2, 10).wait()
 
 
-def finish(back_ref, coords_ref, own_ref, pick_ref, wdst_ref, force_ref, grad_ref):
-    pick_t = pick_ref[...]
-    lines = jnp.concatenate([back_ref[...].astype(BF16), corner_lines(coords_ref)], axis=0)
+def finish(
+    back_hbm,
+    coords_hbm,
+    pick_hbm,
+    own_hbm,
+    wdst_hbm,
+    force_hbm,
+    grad_hbm,
+    back_v,
+    coords_v,
+    pick_v,
+    own_v,
+    wdst_v,
+    force_v,
+    grad_v,
+    sems,
+):
+    sources = (back_hbm, coords_hbm, pick_hbm, own_hbm, wdst_hbm)
+    targets = (back_v, coords_v, pick_v, own_v, wdst_v)
+    loads = [pltpu.make_async_copy(a, b, sems.at[step]) for step, (a, b) in enumerate(zip(sources, targets))]
+    for copy in loads:
+        copy.start()
+    for copy in loads:
+        copy.wait()
+    pick_t = pick_v[...]
+    lines = jnp.concatenate([back_v[...].astype(BF16), corner_lines(coords_v)], axis=0)
     returned = mm(pick_t, lines).astype(BF16)
-    grad_ref[...] = own_ref[0:ATOMS, :] + nt(returned, wdst_ref[...])
-    total8 = own_ref[ATOMS:, :] + sum_pieces(nt(split_rows(unpack_coords(coords_ref), 2), pick_t), 2)
-    force_ref[...] = -total8[4:7]
+    total8 = own_v[ATOMS:, :] + sum_pieces(nt(split_rows(unpack_coords(coords_v), 2), pick_t), 2)
+    force_v[...] = -total8[4:7]
+    force_out = pltpu.make_async_copy(force_v, force_hbm, sems.at[5])
+    force_out.start()
+    grad_v[...] = own_v[0:ATOMS, :] + nt(returned, wdst_v[...])
+    grad_out = pltpu.make_async_copy(grad_v, grad_hbm, sems.at[6])
+    grad_out.start()
+    force_out.wait()
+    grad_out.wait()
 
 
 def body(
@@ -548,7 +577,6 @@
         weight_readout.reshape(1, CH),
     ]
     hbm = pl.BlockSpec(memory_space=pltpu.HBM)
-    vmem = pl.BlockSpec(memory_space=pltpu.VMEM)
     back, coords, own, pick_t = pl.pallas_call(
         kernel,
         out_shape=(
@@ -585,11 +613,21 @@
             jax.ShapeDtypeStruct((3, ATOMS), F32),
             jax.ShapeDtypeStruct((ATOMS, CH), F32),
         ),
-        in_specs=[vmem] * 5,
-        out_specs=(vmem, vmem),
+        in_specs=[hbm] * 5,
+        out_specs=(hbm, hbm),
+        scratch_shapes=[
+            pltpu.VMEM((CORNERS_AT, CH), F32),
+            pltpu.VMEM((COORDS, CH), F32),
+            pltpu.VMEM((ATOMS, SLOTS), BF16),
+            pltpu.VMEM((ATOMS + 8, CH), F32),
+            pltpu.VMEM((CH, CH), BF16),
+            pltpu.VMEM((3, ATOMS), F32),
+            pltpu.VMEM((ATOMS, CH), F32),
+            pltpu.SemaphoreType.DMA((7,)),
+        ],
         compiler_params=pltpu.CompilerParams(vmem_limit_bytes=VMEM),
         name="finish",
-    )(back, coords, own, pick_t, weight_dst)
+    )(back, coords, pick_t, own, weight_dst)
 
 
 def solution(mesh):

time: 32.1 us -> 32.3 us (level)
  no operation moved by 1% of the time
where the time goes in v10:
time: 32.3 us; the launch traced here: 32.2 us
  Pallas kernels  30.9 us (96%)
  between operations  1.29 us (4%)
    pallas_call x1, Pallas kernels, body(): pl.pallas_call(kernel, out_shape=(jax.ShapeDtypeStruct((CORNERS_AT, CH),...  28.8 us
    pallas_call x1, Pallas kernels, body(): pl.pallas_call(finish, out_shape=(jax.ShapeDtypeStruct((3, ATOMS), F32),...  2.11 us

profile of v10, /device:TPU:1, one launch (start us, length us, event | category | flops | bytes accessed | tf_op | source)
XLA Modules:
  0.0 32.2 jit_solution(17451743054269580828)
XLA Ops:
  1.3 28.8 %allegro.1 = (f32[576,128]{1,0:T(8,128)}, f32[208,128]{1,0:T(8,128)}, f32[136,128]{1,0:T(8,128)}, bf16[128,640]{1,0:T(8,128)(2,1)}) custom-call(s32[1,27]{1,0:T(1,128)} %prefix_hbm.1, s32[1,1]{1,0:T(1,128)} %bitcast.2.fill_hbm, f32[128,128]{1,0:T(8,128)} %feat_hbm.1, f32[3,128]{1,0:T(4,128)} %pos_hbm.1, s32[1,608]{1,0:T(1,128)} %send_hbm.1, ...), custom_call_target="tpu_custom_call" | custom-call | tf_op jit(solution)/shard_map/allegro/pallas_call | solution.py:580
  30.0 2.1 %finish.1 = (f32[3,128]{1,0:T(4,128)}, f32[128,128]{1,0:T(8,128)}) custom-call(f32[576,128]{1,0:T(8,128)} %get-tuple-element.6.back_hbm, f32[208,128]{1,0:T(8,128)} %get-tuple-element.7.coords_hbm, bf16[128,640]{1,0:T(8,128)(2,1)} %get-tuple-element.8.pick_hbm, f32[136,128]{1,0:T(8,128)} %get-tuple-element.9.own_hbm, bf16[128,128]{1,0:T(8,128)(2,1)} %wdst_hbm.3), custom_call_target="tpu_custom_call" | custom-call | tf_op jit(solution)/shard_map/finish/pallas_call | solution.py:610

commit v11 on v9

--- a/solution.py
+++ b/solution.py
@@ -215,12 +215,7 @@
     dmixed = mm(w["mix"], dupd)
     dlatent = dupdated + dmixed[:CH] + mm(side_by_side(dmixed[CH:].astype(BF16)), kernels)
     dpre = (dlatent * env).astype(BF16) * dact
-    b1, b2 = near_far[CH : 2 * CH], near_far[2 * CH :]
-    dupd_t = dupd.T
-    pairs = [
-        (jnp.concatenate([dupd_t, b.T], axis=1), jnp.concatenate([b, dupd], axis=0)) for b in (b1, b2)
-    ]
-    return dpre, (dlatent, act, hid_act, pairs)
+    return dpre, (dlatent, act, hid_act, near_far, dupd)
 
 
 def slot_ids_across(dst_row):
@@ -239,11 +234,15 @@
 
 
 def edge_coords(dpre, kept, geo, same, w):
-    dlatent, act, hid_act, pairs = kept
+    dlatent, act, hid_act, near_far, dupd = kept
     r3, r15, r5 = math.sqrt(3.0), math.sqrt(15.0), math.sqrt(5.0)
     qx, qy, qz = geo["q"]
     denv = jnp.sum(hid_act * w["ro"] + dlatent * act, axis=0, keepdims=True)
-    t1, t2 = (mm(*pair).astype(BF16) * same for pair in pairs)
+    dupd_t = dupd.T
+    t1, t2 = (
+        mm(jnp.concatenate([dupd_t, b.T], axis=1), jnp.concatenate([b, dupd], axis=0)).astype(BF16) * same
+        for b in (near_far[CH : 2 * CH], near_far[2 * CH :])
+    )
     dy1 = mm(geo["left1"], t1)
     dy1 = dy1[0:8] + dy1[16:24]
     dy2 = mm(geo["left2"], t2)

time: 32.1 us -> 32.1 us (level)
  no operation moved by 1% of the time
where the time goes in v11:
time: 32.1 us; the launch traced here: 32 us
  Pallas kernels  30.7 us (96%)
  between operations  1.29 us (4%)
    pallas_call x1, Pallas kernels, body(): pl.pallas_call(kernel, out_shape=(jax.ShapeDtypeStruct((CORNERS_AT, CH),...  28.6 us
    pallas_call x1, Pallas kernels, body(): pl.pallas_call(finish, out_shape=(jax.ShapeDtypeStruct((3, ATOMS), F32),...  2.07 us

profile of v11, /device:TPU:1, one launch (start us, length us, event | category | flops | bytes accessed | tf_op | source)
XLA Modules:
  0.0 32.0 jit_solution(7448992628255941714)
XLA Ops:
  1.3 28.6 %allegro.1 = (f32[576,128]{1,0:T(8,128)}, f32[208,128]{1,0:T(8,128)}, f32[136,128]{1,0:T(8,128)}, bf16[128,640]{1,0:T(8,128)(2,1)}) custom-call(s32[1,27]{1,0:T(1,128)} %prefix_hbm.1, s32[1,1]{1,0:T(1,128)} %bitcast.2.fill_hbm, f32[128,128]{1,0:T(8,128)} %feat_hbm.1, f32[3,128]{1,0:T(4,128)} %pos_hbm.1, s32[1,608]{1,0:T(1,128)} %send_hbm.1, ...), custom_call_target="tpu_custom_call" | custom-call | tf_op jit(solution)/shard_map/allegro/pallas_call | solution.py:551
  29.9 2.1 %finish.1 = (f32[3,128]{1,0:T(4,128)}, f32[128,128]{1,0:T(8,128)}) custom-call(f32[576,128]{1,0:T(8,128)} %get-tuple-element.6.back_ref, f32[208,128]{1,0:T(8,128)} %get-tuple-element.7.coords_ref, f32[136,128]{1,0:T(8,128)} %get-tuple-element.8.own_ref, bf16[128,640]{1,0:T(8,128)(2,1)} %get-tuple-element.9.pick_ref, bf16[128,128]{1,0:T(8,128)(2,1)} %wdst_ref.1), custom_call_target="tpu_custom_call" | custom-call | tf_op jit(solution)/shard_map/finish/pallas_call | solution.py:581

commit v12 on v9

--- a/solution.py
+++ b/solution.py
@@ -484,10 +484,11 @@
     far = nt(w["dst_t"], in1[0:LINES_AT, :].astype(BF16)).astype(BF16)
     dpre, kept = edge_pass(pre_known + mm(far, ghost[:LINES_AT]), geo, w)
 
-    some = nt(ghost[LINES_AT:], dpre)
+    back = nt(ghost, dpre)
+    some = back[LINES_AT:]
     out2[LINES_AT:, :] = some[: CORNERS_AT - LINES_AT]
     send_lines(LINES, out2, in2, 6, -1)
-    out2[0:LINES_AT, :] = nt(ghost[:LINES_AT], dpre)
+    out2[0:LINES_AT, :] = back[:LINES_AT]
     send_lines(FACES, out2, in2, 8, -1)
     dq_pieces = split_rows(edge_coords(dpre, kept, geo, same, w), 2)
     store_coords(coords_out2, sum_pieces(mm(dq_pieces, ghost_t), 2), some[CORNERS_AT - LINES_AT :], False)

time: 32.1 us -> 32.2 us (level)
  no operation moved by 1% of the time
where the time goes in v12:
time: 32.2 us; the launch traced here: 32 us
  Pallas kernels  30.7 us (95%)
  between operations  1.29 us (4%)
    pallas_call x1, Pallas kernels, body(): pl.pallas_call(kernel, out_shape=(jax.ShapeDtypeStruct((CORNERS_AT, CH),...  28.6 us
    pallas_call x1, Pallas kernels, body(): pl.pallas_call(finish, out_shape=(jax.ShapeDtypeStruct((3, ATOMS), F32),...  2.07 us

profile of v12, /device:TPU:1, one launch (start us, length us, event | category | flops | bytes accessed | tf_op | source)
XLA Modules:
  0.0 32.0 jit_solution(16560130530930942237)
XLA Ops:
  1.3 28.6 %allegro.1 = (f32[576,128]{1,0:T(8,128)}, f32[208,128]{1,0:T(8,128)}, f32[136,128]{1,0:T(8,128)}, bf16[128,640]{1,0:T(8,128)(2,1)}) custom-call(s32[1,27]{1,0:T(1,128)} %prefix_hbm.1, s32[1,1]{1,0:T(1,128)} %bitcast.2.fill_hbm, f32[128,128]{1,0:T(8,128)} %feat_hbm.1, f32[3,128]{1,0:T(4,128)} %pos_hbm.1, s32[1,608]{1,0:T(1,128)} %send_hbm.1, ...), custom_call_target="tpu_custom_call" | custom-call | tf_op jit(solution)/shard_map/allegro/pallas_call | solution.py:553
  29.9 2.1 %finish.1 = (f32[3,128]{1,0:T(4,128)}, f32[128,128]{1,0:T(8,128)}) custom-call(f32[576,128]{1,0:T(8,128)} %get-tuple-element.6.back_ref, f32[208,128]{1,0:T(8,128)} %get-tuple-element.7.coords_ref, f32[136,128]{1,0:T(8,128)} %get-tuple-element.8.own_ref, bf16[128,640]{1,0:T(8,128)(2,1)} %get-tuple-element.9.pick_ref, bf16[128,128]{1,0:T(8,128)(2,1)} %wdst_ref.1), custom_call_target="tpu_custom_call" | custom-call | tf_op jit(solution)/shard_map/finish/pallas_call | solution.py:583
